TPU v7x, 32 devices: a whole 2x2x4 slice. The times are simulated.
32 devices in a mesh: dp: 2 (over y), owner: 16 (over z, x, core).
Axes of the slice: x: 2, y: 2, z: 4, core: 2. Of those that a mesh axis runs over, the one named last changes fastest.
Arguments:
- partials: bfloat16 [32, 48, 128, 128], P(('dp', 'owner')), may hold values from -1.25 to 1.25
- owners: int32 [48], replicated, may hold values from 0 to 15, as said below
- step_count: int32 [1], replicated, may hold values from 1 to 49
- master: float32 [96, 128, 128], P('owner'), may hold values from -0.3125 to 0.3125
- moment: float32 [96, 128, 128], P('owner'), may hold values from -4 to 4
- second: float32 [96, 128, 128], P('owner'), may hold values from 0.1 to 10
- stat_left: float32 [96, 128, 128], P('owner'), may hold values from -1.5 to 82
- stat_right: float32 [96, 128, 128], P('owner'), may hold values from -1.5 to 82
- basis_left: float32 [96, 128, 128], P('owner'), may hold values from -0.12 to 1.12
- basis_right: float32 [96, 128, 128], P('owner'), may hold values from -0.12 to 1.12
Outputs:
- weights_all: bfloat16 [48, 128, 128], replicated
- direction: float32 [96, 128, 128], P('owner')
- left_new: float32 [96, 128, 128], P('owner')
- right_new: float32 [96, 128, 128], P('owner')
Inputs may be any that keep to these rules, and one draw needn't show every extreme that they name: `owners`: each owner index is named by at least one and at most 6 blocks, and some index by exactly 6.
All inputs are finite; a program needn't handle non-finite values.
Results may differ from a plain program's by a relative error of at most 0.0065.
Values may be sent and summed in bfloat16 or wider, within the bound.
No kernel may reach another device: no remote copies, remote signals or barrier semaphores. Data moves between devices by JAX's collectives and lax.ppermute only.
A program may use at most 128 MiB of HBM per device.

v0:
```python
import jax
import jax.numpy as jnp
from jax import lax
from jax.sharding import PartitionSpec as P

NS_ITERS = 6


def product(left, right):
    return jnp.matmul(left, right, precision=lax.Precision.HIGHEST)


def transposed(array):
    return jnp.swapaxes(array, 1, 2)


def refresh(stat, basis):
    power = product(stat, basis)
    magnitude = jnp.sqrt(jnp.sum(power * power, axis=(1, 2), keepdims=True))
    iterate = power / (magnitude + 1e-06)
    for repeat_count in range(NS_ITERS):
        iterate = 1.5 * iterate - 0.5 * product(iterate, product(transposed(iterate), iterate))
    return iterate


def slot_layout(owners, slot_count, total_slot_count):
    block_count = owners.shape[0]
    slot_position = jnp.arange(block_count, dtype=jnp.int32)
    before = (owners[:, None] == owners[None, :]) & (
        slot_position[:, None] > slot_position[None, :]
    )
    rank_in = jnp.sum(before.astype(jnp.int32), axis=1)
    target = owners * slot_count + rank_in
    matches = (target[:, None] == jnp.arange(total_slot_count, dtype=jnp.int32)[None, :]).astype(
        jnp.int32
    )
    source = jnp.sum(matches * slot_position[:, None], axis=0)
    occupied = jnp.sum(matches, axis=0)
    return (target, source, occupied)


def soap_update(
    gradient, occupied, moment, second, stat_left, stat_right, basis_left, basis_right, step_count
):
    elapsed = step_count[0].astype(jnp.float32)
    moment_new = 0.95 * moment + 0.05 * gradient
    rotated = product(transposed(basis_left), product(gradient, basis_right))
    rot_moment = product(transposed(basis_left), product(moment_new, basis_right))
    second_new = 0.95 * second + 0.05 * rotated * rotated
    correction = 1.0 - jnp.power(jnp.float32(0.95), elapsed)
    scaled = rot_moment / correction / (jnp.sqrt(second_new / correction) + 1e-08)
    occupied_mask = (occupied > 0)[:, None, None]
    direction = jnp.where(
        occupied_mask, product(basis_left, product(scaled, transposed(basis_right))), 0.0
    )
    left_stat = 0.95 * stat_left + 0.05 * product(gradient, transposed(gradient))
    right_stat = 0.95 * stat_right + 0.05 * product(transposed(gradient), gradient)
    left_new = jnp.where(occupied_mask, refresh(left_stat, basis_left), basis_left)
    right_new = jnp.where(occupied_mask, refresh(right_stat, basis_right), basis_right)
    return (direction, left_new, right_new)


def body(
    partials,
    owners,
    step_count,
    master,
    moment,
    second,
    stat_left,
    stat_right,
    basis_left,
    basis_right,
):
    owner_count = lax.axis_size("owner")
    slot_count = master.shape[0]
    total_slot_count = slot_count * owner_count
    target, source, occupied = slot_layout(owners, slot_count, total_slot_count)
    first_slot = lax.axis_index("owner") * slot_count
    occupied_mine = lax.dynamic_slice_in_dim(occupied, first_slot, slot_count, 0)
    own_part = partials[0]
    mask_all = (occupied > 0).astype(jnp.float32)[:, None, None]
    placed = jnp.take(own_part, source, axis=0).astype(jnp.float32) * mask_all
    summed = lax.psum_scatter(placed.astype(jnp.bfloat16), "owner", scatter_dimension=0, tiled=True)
    gradient = lax.psum(summed, "dp").astype(jnp.float32)
    direction, left_new, right_new = soap_update(
        gradient,
        occupied_mine,
        moment,
        second,
        stat_left,
        stat_right,
        basis_left,
        basis_right,
        step_count,
    )
    updated = (master - 0.01 * (direction + 0.1 * master)).astype(jnp.bfloat16)
    every_slot = lax.all_gather(updated, "owner", axis=0, tiled=True)
    weights_all = jnp.take(every_slot, target, axis=0)
    return (weights_all, direction, left_new, right_new)


def solution(mesh):
    placed = (
        P(("dp", "owner"), None, None, None),
        P(),
        P(),
        P("owner", None, None),
        P("owner", None, None),
        P("owner", None, None),
        P("owner", None, None),
        P("owner", None, None),
        P("owner", None, None),
        P("owner", None, None),
    )
    return jax.shard_map(
        body,
        mesh=mesh,
        in_specs=placed,
        out_specs=(P(), P("owner", None, None), P("owner", None, None), P("owner", None, None)),
        check_vma=False,
    )
```

profile of v0, /device:TPU:0, one launch (start us, length us, event | category | flops | bytes accessed | tf_op | source)
XLA Modules:
  0.0 180.1 jit_solution(31442569773386312)
XLA Ops:
  7.2 1.0 convert_reduce_fusion.1
  9.0 2.7 %gather_fusion = bf16[96,128,128]{2,1,0:T(8,128)(2,1)} fusion(bf16[48,128,128]{2,1,0:T(8,128)(2,1)S(1)} %bitcast.87, s32[1024]{0:T(1024)S(1)} %pad_clamp_fusion.1), kind=kCustom, calls=%fused_computation | custom fusion | bytes 6291840 | tf_op jit(solution)/shard_map/jit(_take)/gather | solution.py:83
  11.7 4.7 %copy.70 = bf16[96,128,128]{1,2,0:T(8,128)(2,1)} copy(bf16[96,128,128]{2,1,0:T(8,128)(2,1)} %gather_fusion) | data formatting | bytes 6291456 | tf_op jit(solution)/shard_map/jit(_take)/gather | solution.py:83
  16.3 4.5 %multiply_convert_fusion = bf16[96,128,128]{1,2,0:T(8,128)(2,1)} fusion(f32[96]{0:T(128)S(1)} %get-tuple-element.30, bf16[96,128,128]{1,2,0:T(8,128)(2,1)} %copy.70, pred[96]{0:T(512)(128)(4,1)S(1)} %get-tuple-element.31), kind=kLoop, calls=%fused_computation.2 | loop fusion | flops 6291456 | bytes 6291936 | tf_op jit(solution)/shard_map/convert_element_type | solution.py:84
  20.9 0.9 copy-done.5
  22.2 2.0 %copy.73 = f32[6,128,128]{1,2,0:T(8,128)} copy(f32[6,128,128]{2,1,0:T(8,128)} %param.15) | data formatting | bytes 786432 | tf_op args[5]
  24.8 1.2 copy.69
  26.0 1.9 %copy.79 = f32[6,128,128]{1,2,0:T(8,128)} copy(f32[6,128,128]{2,1,0:T(8,128)} %param.13) | data formatting | bytes 786432 | tf_op args[3]
  27.9 62.0 %reduce-scatter.2.cloned.1.call-done = bf16[6,128,128]{1,2,0:T(8,128)(2,1)} async-done(((bf16[96,128,128]{1,2,0:T(8,128)(2,1)}), bf16[6,128,128]{1,2,0:T(8,128)(2,1)}) %reduce-scatter.2.cloned.1.call-update) | async-done | bytes 196624 | tf_op jit(solution)/shard_map/reduce_scatter | solution.py:84
  90.3 23.2 %all-reduce.2.cloned.1.call-done = bf16[6,128,128]{1,2,0:T(8,128)(2,1)} async-done(((bf16[6,128,128]{1,2,0:T(8,128)(2,1)}), bf16[6,128,128]{1,2,0:T(8,128)(2,1)}) %all-reduce.2.cloned.1.call-update) | async-done | bytes 196624 | tf_op jit(solution)/shard_map/psum | solution.py:85
  113.4 1.3 fusion.2
  114.8 1.6 multiply_reduce_fusion
  117.0 1.3 fusion.1
  118.3 0.9 multiply_reduce_fusion.1
  122.3 1.0 subtract_convert_fusion
  123.2 0.8 copy.80
  124.1 2.9 %fusion.31 = f32[6,128,128]{2,1,0:T(8,128)} fusion(f32[6,128,128]{2,1,0:T(8,128)} %get-tuple-element.29, f32[6]{0:T(128)} %sqrt_add_fusion), kind=kOutput, calls=%fused_computation.58 | convolution fusion | flops 151093248 | bytes 786456 | tf_op jit(solution)/shard_map/dot_general | solution.py:10
  127.5 0.9 copy.102
  128.4 1.6 fusion.30
  130.0 1.6 fusion.9
  131.6 0.8 fusion.43
  133.0 0.8 fusion.44
  134.4 0.8 fusion.45
  136.0 0.8 fusion.46
  137.4 0.8 fusion.47
  143.0 0.8 fusion.41
  144.4 0.8 fusion.42
  145.2 1.3 fusion.4
  146.5 1.3 fusion.11
  147.8 21.6 %all-gather.2.cloned.1.call-done = bf16[96,128,128]{2,1,0:T(8,128)(2,1)} async-done(((bf16[6,128,128]{2,1,0:T(8,128)(2,1)}), bf16[96,128,128]{2,1,0:T(8,128)(2,1)}) %all-gather.2.cloned.1.call-update) | async-done | bytes 3145744 | tf_op jit(solution)/shard_map/all_gather | solution.py:98
  169.4 2.7 %gather_fusion.1 = bf16[48,128,128]{2,1,0:T(8,128)(2,1)S(1)} fusion(bf16[96,128,128]{2,1,0:T(8,128)(2,1)} %all-gather.2.cloned.1.call-done, s32[1024]{0:T(1024)S(1)} %pad_clamp_fusion), kind=kCustom, calls=%fused_computation.1 | custom fusion | bytes 3145920 | tf_op jit(solution)/shard_map/jit(_take)/gather | solution.py:99
  172.2 1.4 broadcast_select_fusion
  (54 shorter events, 13.5 us)
Async XLA Ops:
  7.2 1.8 %copy-start = (bf16[1,48,128,128]{3,2,1,0:T(8,128)(2,1)S(1)}, bf16[1,48,128,128]{3,2,1,0:T(8,128)(2,1)}, u32[]{:S(2)}) copy-start(bf16[1,48,128,128]{3,2,1,0:T(8,128)(2,1)} %param.10) | copy-start | bytes 4718596
  7.2 82.8 %reduce-scatter.2.cloned.1.call-start = ((), (), s32[]{:S(2)}) async-start(), calls=%async_computation.1 | async-start | bytes 3342336 | tf_op jit(solution)/shard_map/reduce_scatter | solution.py:84
  20.8 1.0 copy-start.5
  20.8 1.2 copy-start.6
  20.8 93.9 %copy-start.1 = (f32[6,128,128]{2,1,0:T(8,128)S(1)}, f32[6,128,128]{2,1,0:T(8,128)}, u32[]{:S(2)}) copy-start(f32[6,128,128]{2,1,0:T(8,128)} %param.19) | copy-start | bytes 1179652
  20.9 92.6 %all-reduce.2.cloned.1.call-start = ((), (), s32[]{:S(2)}) async-start(), calls=%async_computation.2 | async-start | bytes 393216 | tf_op jit(solution)/shard_map/psum | solution.py:85
  22.2 96.1 %copy-start.3 = (f32[6,128,128]{2,1,0:T(8,128)S(1)}, f32[6,128,128]{2,1,0:T(8,128)}, u32[]{:S(2)}) copy-start(f32[6,128,128]{2,1,0:T(8,128)} %param.18) | copy-start | bytes 1179652
  90.0 79.5 %all-gather.2.cloned.1.call-start = ((), (), s32[]{:S(2)}) async-start(), calls=%async_computation.3 | async-start | bytes 3342336 | tf_op jit(solution)/shard_map/all_gather | solution.py:98
  113.4 5.7 %copy-start.2 = (bf16[6,128,128]{1,2,0:T(8,128)(2,1)S(1)}, bf16[6,128,128]{1,2,0:T(8,128)(2,1)}, u32[]{:S(2)}) copy-start(bf16[6,128,128]{1,2,0:T(8,128)(2,1)} %all-reduce.2.cloned.1.call-done) | copy-start | bytes 589828
  113.4 6.3 %copy-start.7 = (f32[6,128,128]{1,2,0:T(8,128)S(1)}, f32[6,128,128]{1,2,0:T(8,128)}, u32[]{:S(2)}) copy-start(f32[6,128,128]{1,2,0:T(8,128)} %copy.73) | copy-start | bytes 1179652
  119.7 2.6 %copy-start.4 = (f32[6,128,128]{1,2,0:T(8,128)S(1)}, f32[6,128,128]{1,2,0:T(8,128)}, u32[]{:S(2)}) copy-start(f32[6,128,128]{1,2,0:T(8,128)} %copy.79) | copy-start | bytes 1179652
  124.1 5.9 %copy-start.8 = (f32[6,128,128]{2,1,0:T(8,128)S(1)}, f32[6,128,128]{2,1,0:T(8,128)}, u32[]{:S(2)}) copy-start(f32[6,128,128]{2,1,0:T(8,128)} %get-tuple-element.29) | copy-start | bytes 1179652
  134.4 3.8 %copy-start.9 = (f32[6]{0:T(128)S(1)}, f32[6]{0:T(128)}, u32[]{:S(2)}) copy-start(f32[6]{0:T(128)} %sqrt_add_fusion.1) | copy-start | bytes 76
Sparse Core Ops, SparseCore 0:
  21.0 68.9 reduce-scatter.1
  92.2 21.1 all-reduce.1
  124.2 45.1 all-gather.1
where the time goes:
time: 181 us; the launch traced here: 180 us
  waiting for transfers between devices  107 us (59%)
  matrix products  31.2 us (17%)
  local copies, waits for them, and re-layouts  18.1 us (10%)
  between operations  14.8 us (8%)
  other arithmetic  8.79 us (5%)
    reduce_scatter x1, waiting for transfers between devices, body(): lax.psum_scatter(placed.astype(jnp.bfloat16), 'owner', scatter_dimension=...  62 us
    dot_general x34, matrix products, product(): return jnp.matmul(left, right, precision=lax.Precision.HIGHEST)  31.2 us
    psum x1, waiting for transfers between devices, body(): gradient = lax.psum(summed, 'dp').astype(jnp.float32)  23.2 us
    all_gather x1, waiting for transfers between devices, body(): every_slot = lax.all_gather(updated, 'owner', axis=0, tiled=True)  21.6 us
    gather x2, local copies, waits for them, and re-layouts, body(): placed = jnp.take(own_part, source, axis=0).astype(jnp.float32) * mask_all  7.35 us
    unnamed x26, local copies, waits for them, and re-layouts  7.22 us
    convert_element_type x1, other arithmetic, body(): placed.astype(jnp.bfloat16)  4.48 us
  transfers between devices with their start and end apart: 3, of which 3 were waited for; matrix products, arithmetic and copies ran while one was open for 16% of the time, Pallas kernels for 0%

commit v1 on v0

v1 whole, which is shorter than its diff:
```python
import functools

import jax
import jax.numpy as jnp
from jax import lax
from jax.experimental import pallas as pl
from jax.experimental.pallas import tpu as pltpu
from jax.sharding import PartitionSpec as P

NS_ITERS = 6
AXES = ("dp", "owner")
F32 = jnp.float32
BF16 = jnp.bfloat16
VMEM_LIMIT = 48 * 1024 * 1024
VMEM = pl.BlockSpec(memory_space=pltpu.VMEM)
SMEM = pl.BlockSpec(memory_space=pltpu.SMEM)


def shape(dims, dtype):
    return jax.ShapeDtypeStruct(dims, dtype)


def call(kernel, scalars, arrays, outs, flops=0):
    moved = sum(a.size * a.dtype.itemsize for a in list(arrays) + list(outs))
    return pl.pallas_call(
        kernel,
        out_shape=tuple(outs),
        in_specs=[SMEM] * len(scalars) + [VMEM] * len(arrays),
        out_specs=tuple(VMEM for _ in outs),
        compiler_params=pltpu.CompilerParams(vmem_limit_bytes=VMEM_LIMIT),
        cost_estimate=pl.CostEstimate(flops=flops, bytes_accessed=moved, transcendentals=0),
    )(*scalars, *arrays)


class Grid:
    def __init__(self, dp_count, owner_count):
        self.dp, self.core = dp_count, 2
        self.high = 4
        self.middle = owner_count // (self.core * self.high)
        self.owners = owner_count

    def place(self):
        owner = lax.axis_index("owner")
        return jnp.stack(
            [
                lax.axis_index("dp"),
                owner // (self.core * self.middle),
                owner // self.core % self.middle,
                owner % self.core,
            ]
        ).astype(jnp.int32)

    def swap(self, array, dp=0, high=0, middle=0, core=0):
        step = (high * self.middle + middle) * self.core + core
        pairs = [
            (d * self.owners + o, (d ^ dp) * self.owners + (o ^ step))
            for d in range(self.dp)
            for o in range(self.owners)
        ]
        return lax.ppermute(array, AXES, pairs)


def split(value):
    top = value.astype(BF16)
    return top, (value - top.astype(F32)).astype(BF16)


def dot(left, right, dims):
    return lax.dot_general(left, right, (dims, ((), ())), preferred_element_type=F32)


NN = ((1,), (0,))
NT = ((1,), (1,))
TN = ((0,), (0,))


def product(left, right, dims=NN):
    (left_top, left_low), (right_top, right_low) = left, right
    small = dot(left_low, right_top, dims) + dot(left_top, right_low, dims)
    return dot(left_top, right_top, dims) + small


def spread_kernel(grid, slots, place, owners, rank, own, other, *outs):
    rows = own.shape[1] // grid.dp
    dp, middle, core = place[0], place[2], place[3]

    def step(block, carry):
        owner = owners[block]
        high_of = owner // (grid.core * grid.middle)
        middle_of = owner // grid.core % grid.middle
        at = high_of * slots + rank[block]

        @pl.when(owner % grid.core == core)
        def _():
            for dm in range(grid.middle):

                @pl.when(middle_of == middle ^ dm)
                def _():
                    for dd in range(grid.dp):
                        part = pl.ds(pl.multiple_of((dp ^ dd) * rows, rows), rows)
                        total = own[block, part].astype(F32) + other[block, part].astype(F32)
                        outs[dm * grid.dp + dd][at] = total.astype(BF16)

        return carry

    lax.fori_loop(0, own.shape[0], step, 0)


def gather_sum_kernel(grid, slots, place, *refs):
    count = grid.middle * grid.dp
    arrays, outs = refs[:count], refs[count:]
    for dh in range(grid.high):
        first = (place[1] ^ dh) * slots
        for slot in range(slots):
            total = arrays[0][first + slot].astype(F32)
            for array in arrays[1:]:
                total = total + array[first + slot].astype(F32)
            outs[dh][slot] = total.astype(BF16)


def sum_kernel(*refs):
    arrays, out = refs[:-1], refs[-1]
    for slot in range(out.shape[0]):
        total = arrays[0][slot].astype(F32)
        for array in arrays[1:]:
            total = total + array[slot].astype(F32)
        out[slot] = total.astype(BF16)


def moment_kernel(moment, left, right, out):
    for slot in range(out.shape[0]):
        half = product(split(moment[slot]), split(right[slot]))
        out[slot] = product(split(left[slot]), split(half), TN)


def step_kernel(grid, place, held, correction, *refs):
    parts = refs[: grid.dp]
    rot_old, second, master, left, right, gradient, direction, updated = refs[grid.dp :]
    slots, rows = parts[0].shape[:2]
    dp = place[0]
    c = correction[0]
    for dd in range(grid.dp):
        part = pl.ds(pl.multiple_of((dp ^ dd) * rows, rows), rows)
        gradient[:, part, :] = parts[dd][...]
    mine = pl.ds(pl.multiple_of(dp * rows, rows), rows)
    for slot in range(slots):
        live = slot < held[0]
        right_top, right_low = split(right[slot])
        left_parts = split(left[slot])
        half = dot(gradient[slot], right_top, NN) + dot(gradient[slot], right_low, NN)
        rotated = product(left_parts, split(half), TN)
        rot_moment = 0.95 * rot_old[slot] + 0.05 * rotated
        second_new = 0.95 * second[slot] + 0.05 * rotated * rotated
        scaled = rot_moment / c / (jnp.sqrt(second_new / c) + 1e-08)
        turned = product(split(scaled), (right_top, right_low), NT)
        moved = product(left_parts, split(turned))
        direction[slot] = jnp.where(live, moved, 0.0)
        weights = master[slot, mine]
        updated[slot] = (weights - 0.01 * (direction[slot, mine] + 0.1 * weights)).astype(BF16)


def refresh_kernel(dims, held, gradient, stat, basis, out):
    slots = out.shape[0]
    for slot in range(slots):
        gram = dot(gradient[slot], gradient[slot], dims)
        power = product(split(0.95 * stat[slot] + 0.05 * gram), split(basis[slot]))
        out[slot] = power / (jnp.sqrt(jnp.sum(power * power)) + 1e-06)

    def step(_, carry):
        for slot in range(slots):
            iterate = out[slot]
            parts = split(iterate)
            square = product(parts, parts, TN)
            out[slot] = 1.5 * iterate - 0.5 * product(parts, split(square))
        return carry

    lax.fori_loop(0, NS_ITERS, step, 0)
    for slot in range(slots):
        out[slot] = jnp.where(slot < held[0], out[slot], basis[slot])


def join_kernel(grid, place, *refs):
    arrays, out = refs[:-1], refs[-1]
    slots = arrays[0].shape[0]
    for dh in range(grid.high):
        first = (place[1] ^ dh) * slots
        for slot in range(slots):
            out[first + slot] = arrays[dh][slot]


def weights_kernel(grid, slots, place, owners, rank, *refs):
    arrays, out = refs[:-1], refs[-1]
    rows = arrays[0].shape[1]
    dp, middle, core = place[0], place[2], place[3]

    def step(block, carry):
        owner = owners[block]
        at = owner // (grid.core * grid.middle) * slots + rank[block]
        for dc in range(grid.core):
            for dm in range(grid.middle):
                from_core = owner % grid.core == core ^ dc
                from_middle = owner // grid.core % grid.middle == middle ^ dm

                @pl.when(from_core & from_middle)
                def _():
                    for dd in range(grid.dp):
                        part = pl.ds(pl.multiple_of((dp ^ dd) * rows, rows), rows)
                        out[block, part] = arrays[(dc * grid.middle + dm) * grid.dp + dd][at]

        return carry

    lax.fori_loop(0, out.shape[0], step, 0)


def body(
    partials,
    owners,
    step_count,
    master,
    moment,
    second,
    stat_left,
    stat_right,
    basis_left,
    basis_right,
):
    grid = Grid(lax.axis_size("dp"), lax.axis_size("owner"))
    slots, size = master.shape[:2]
    blocks = owners.shape[0]
    rows = size // grid.dp
    place = grid.place()
    position = jnp.arange(blocks, dtype=jnp.int32)
    earlier = (owners[:, None] == owners[None, :]) & (position[:, None] > position[None, :])
    rank = jnp.sum(earlier.astype(jnp.int32), axis=1)
    held = jnp.sum((owners == lax.axis_index("owner")).astype(jnp.int32))[None]
    correction = 1.0 - jnp.power(jnp.float32(0.95), step_count.astype(F32))

    share = shape((slots, rows, size), BF16)
    column = shape((grid.high * slots, rows, size), BF16)
    state = shape((slots, size, size), F32)
    plane = [(dm, dd) for dm in range(grid.middle) for dd in range(grid.dp)]

    own = partials[0]
    other = grid.swap(own, core=1)
    sent = call(
        functools.partial(spread_kernel, grid, slots),
        (place, owners, rank),
        (own, other),
        [column] * len(plane),
    )
    got = [sent[0]] + [
        grid.swap(a, middle=dm, dp=dd) for a, (dm, dd) in zip(sent[1:], plane[1:], strict=True)
    ]
    (rot_old,) = call(moment_kernel, (), (moment, basis_left, basis_right), [state], 12 * slots * size**3)
    sent = call(
        functools.partial(gather_sum_kernel, grid, slots), (place,), got, [share] * grid.high
    )
    got = [sent[0]] + [grid.swap(sent[dh], high=dh) for dh in range(1, grid.high)]
    (summed,) = call(sum_kernel, (), got, [share])
    parts = [summed] + [grid.swap(summed, dp=dd) for dd in range(1, grid.dp)]
    gradient, direction, updated = call(
        functools.partial(step_kernel, grid),
        (place, held, correction),
        (*parts, rot_old, second, master, basis_left, basis_right),
        [shape((slots, size, size), BF16), state, share],
        22 * slots * size**3,
    )
    cost = 2 * (1 + 3 + 36) * slots * size**3
    (left_new,) = call(
        functools.partial(refresh_kernel, NT), (held,), (gradient, stat_left, basis_left), [state], cost
    )
    (right_new,) = call(
        functools.partial(refresh_kernel, TN), (held,), (gradient, stat_right, basis_right), [state], cost
    )
    got = [updated] + [grid.swap(updated, high=dh) for dh in range(1, grid.high)]
    (joined,) = call(functools.partial(join_kernel, grid), (place,), got, [column])
    got = [joined] + [grid.swap(joined, middle=dm, dp=dd) for dm, dd in plane[1:]]
    got = got + [grid.swap(a, core=1) for a in got]
    (weights_all,) = call(
        functools.partial(weights_kernel, grid, slots),
        (place, owners, rank),
        got,
        [shape((blocks, size, size), BF16)],
    )
    return (weights_all, direction, left_new, right_new)


def solution(mesh):
    placed = (
        P(("dp", "owner"), None, None, None),
        P(),
        P(),
        P("owner", None, None),
        P("owner", None, None),
        P("owner", None, None),
        P("owner", None, None),
        P("owner", None, None),
        P("owner", None, None),
        P("owner", None, None),
    )
    return jax.shard_map(
        body,
        mesh=mesh,
        in_specs=placed,
        out_specs=(P(), P("owner", None, None), P("owner", None, None), P("owner", None, None)),
        check_vma=False,
    )
```

time: 181 us -> 98 us (0.54)
  waiting for transfers between devices: 107 us -> 47.1 us
  matrix products: 31.2 us -> 0 us
  Pallas kernels: 0 us -> 26.5 us
  starting transfers between devices: 0.3 us -> 19 us
  local copies, waits for them, and re-layouts: 18.1 us -> 2.1 us
  between operations: 14.8 us -> 1.46 us
  other arithmetic: 8.79 us -> 1.62 us
    reduce_scatter x1 -> x0, waiting for transfers between devices: 62 us -> none  [body(): lax.psum_scatter(placed.astype(jnp.bfloat16), 'owner', scatter_dimension=...]
    ppermute x0 -> x18, waiting for transfers between devices: none -> 47.1 us  [swap(): return lax.ppermute(array, AXES, pairs)]
    dot_general x34 -> x0, matrix products: 31.2 us -> none  [product(): return jnp.matmul(left, right, precision=lax.Precision.HIGHEST)]
    pallas_call x0 -> x9, Pallas kernels: none -> 26.5 us  [call(): pl.pallas_call(kernel, out_shape=tuple(outs), in_specs=[SMEM] * len(scala...]
    psum x1 -> x0, waiting for transfers between devices: 23.2 us -> none  [body(): gradient = lax.psum(summed, 'dp').astype(jnp.float32)]
    all_gather x1 -> x0, waiting for transfers between devices: 21.6 us -> none  [body(): every_slot = lax.all_gather(updated, 'owner', axis=0, tiled=True)]
    ppermute x0 -> x18, starting transfers between devices: none -> 19 us  [swap(): return lax.ppermute(array, AXES, pairs)]
    gather x3 -> x0, local copies, waits for them, and re-layouts: 10.1 us -> none  [the longest x2 7.35 us: body(): placed = jnp.take(own_part, source, axis=0).astype(jnp.float32) * mask_all]
  transfers between devices with their start and end apart: 3 -> 18, of which waited for: 3 -> 12; matrix products, arithmetic and copies ran while one was open for 16% -> 2% of each run, Pallas kernels for 0% -> 14%
where the time goes in v1:
time: 98 us; the launch traced here: 97.7 us
  waiting for transfers between devices  47.1 us (48%)
  Pallas kernels  26.5 us (27%)
  starting transfers between devices  19 us (19%)
  local copies, waits for them, and re-layouts  2.1 us (2%)
  other arithmetic  1.62 us (2%)
  between operations  1.46 us (1%)
    ppermute x18, waiting for transfers between devices, swap(): return lax.ppermute(array, AXES, pairs)  47.1 us
    pallas_call x9, Pallas kernels, call(): pl.pallas_call(kernel, out_shape=tuple(outs), in_specs=[SMEM] * len(scala...  26.5 us
    ppermute x18, starting transfers between devices, swap(): return lax.ppermute(array, AXES, pairs)  19 us
    unnamed x20, local copies, waits for them, and re-layouts  2.1 us
  transfers between devices with their start and end apart: 18, of which 12 were waited for; matrix products, arithmetic and copies ran while one was open for 2% of the time, Pallas kernels for 14%

profile of v1, /device:TPU:0, one launch (start us, length us, event | category | flops | bytes accessed | tf_op | source)
XLA Modules:
  0.0 97.7 jit_solution(2974024893961319938)
XLA Ops:
  1.2 0.9 convert_reduce_fusion.rank
  2.1 2.3 %collective-permute-done.other = bf16[48,128,128]{2,1,0:T(8,128)(2,1)S(1)} collective-permute-done((bf16[48,128,128]{2,1,0:T(8,128)(2,1)}, bf16[48,128,128]{2,1,0:T(8,128)(2,1)S(1)}, u32[]{:S(2)}, u32[]{:S(2)}) %collective-permute-start) | collective-permute-done | bytes 1572896 | tf_op jit(solution)/shard_map/ppermute | solution.py:60
  4.4 1.4 %copy-done = bf16[1,48,128,128]{3,2,1,0:T(8,128)(2,1)S(1)} copy-done((bf16[1,48,128,128]{3,2,1,0:T(8,128)(2,1)S(1)}, bf16[1,48,128,128]{3,2,1,0:T(8,128)(2,1)}, u32[]{:S(2)}) %copy-start) | copy-done | bytes 1572888
  5.8 0.7 copy-done.6
  6.5 2.0 %shard_map.129 = (bf16[24,64,128]{2,1,0:T(8,128)(2,1)S(1)}, bf16[24,64,128]{2,1,0:T(8,128)(2,1)S(1)}, bf16[24,64,128]{2,1,0:T(8,128)(2,1)S(1)}, bf16[24,64,128]{2,1,0:T(8,128)(2,1)S(1)}) custom-call(s32[4]{0:T(128)S(1)} %pad_add_fusion.place, s32[48]{0:T(128)S(1)} %copy-done.6, s32[48]{0:T(128)S(1)} %convert_reduce_fusion.rank, ...), custom_call_target="tpu_custom_call" | custom-call | bytes 4718592 | tf_op jit(solution)/shard_map/pallas_call | solution.py:25
  8.5 3.0 %collective-permute-start.1 = (bf16[24,64,128]{2,1,0:T(8,128)(2,1)S(1)}, bf16[24,64,128]{2,1,0:T(8,128)(2,1)S(1)}, u32[]{:S(2)}, u32[]{:S(2)}) collective-permute-start(bf16[24,64,128]{2,1,0:T(8,128)(2,1)S(1)} %get-tuple-element.16), channel_id=1, source_target_pairs={{0,16},{1,17},{2,18},{3,19},{4,20},{5,21},{6,22},{7,23},{8,24},{9,... | collective-permute-start | bytes 1179656 | tf_op jit(solution)/shard_map/ppermute | solution.py:60
  11.5 1.5 %collective-permute-start.2 = (bf16[24,64,128]{2,1,0:T(8,128)(2,1)S(1)}, bf16[24,64,128]{2,1,0:T(8,128)(2,1)S(1)}, u32[]{:S(2)}, u32[]{:S(2)}) collective-permute-start(bf16[24,64,128]{2,1,0:T(8,128)(2,1)S(1)} %get-tuple-element.17), channel_id=1, source_target_pairs={{0,2},{1,3},{2,0},{3,1},{4,6},{5,7},{6,4},{7,5},{8,10},{9,11},{10,... | collective-permute-start | bytes 1179656 | tf_op jit(solution)/shard_map/ppermute | solution.py:60
  13.0 7.8 %collective-permute-done.1.refs_1_ = bf16[24,64,128]{2,1,0:T(8,128)(2,1)S(1)} collective-permute-done((bf16[24,64,128]{2,1,0:T(8,128)(2,1)S(1)}, bf16[24,64,128]{2,1,0:T(8,128)(2,1)S(1)}, u32[]{:S(2)}, u32[]{:S(2)}) %collective-permute-start.1) | collective-permute-done | bytes 393248 | tf_op jit(solution)/shard_map/ppermute | solution.py:60
  20.9 2.6 %collective-permute-done.2.refs_2_ = bf16[24,64,128]{2,1,0:T(8,128)(2,1)S(1)} collective-permute-done((bf16[24,64,128]{2,1,0:T(8,128)(2,1)S(1)}, bf16[24,64,128]{2,1,0:T(8,128)(2,1)S(1)}, u32[]{:S(2)}, u32[]{:S(2)}) %collective-permute-start.2) | collective-permute-done | bytes 393248 | tf_op jit(solution)/shard_map/ppermute | solution.py:60
  23.5 7.1 %collective-permute-done.3.refs_3_ = bf16[24,64,128]{2,1,0:T(8,128)(2,1)S(1)} collective-permute-done((bf16[24,64,128]{2,1,0:T(8,128)(2,1)S(1)}, bf16[24,64,128]{2,1,0:T(8,128)(2,1)S(1)}, u32[]{:S(2)}, u32[]{:S(2)}) %collective-permute-start.3) | collective-permute-done | bytes 393248 | tf_op jit(solution)/shard_map/ppermute | solution.py:60
  30.6 0.7 shard_map.130
  31.3 1.8 %collective-permute-start.4 = (bf16[6,64,128]{2,1,0:T(8,128)(2,1)S(1)}, bf16[6,64,128]{2,1,0:T(8,128)(2,1)S(1)}, u32[]{:S(2)}, u32[]{:S(2)}) collective-permute-start(bf16[6,64,128]{2,1,0:T(8,128)(2,1)S(1)} %get-tuple-element.20), channel_id=1, source_target_pairs={{0,4},{1,5},{2,6},{3,7},{4,0},{5,1},{6,2},{7,3},{8,12},{9,13},{10,... | collective-permute-start | bytes 294920 | tf_op jit(solution)/shard_map/ppermute | solution.py:60
  33.1 2.6 %collective-permute-start.5 = (bf16[6,64,128]{2,1,0:T(8,128)(2,1)S(1)}, bf16[6,64,128]{2,1,0:T(8,128)(2,1)S(1)}, u32[]{:S(2)}, u32[]{:S(2)}) collective-permute-start(bf16[6,64,128]{2,1,0:T(8,128)(2,1)S(1)} %get-tuple-element.21), channel_id=1, source_target_pairs={{0,8},{1,9},{2,10},{3,11},{4,12},{5,13},{6,14},{7,15},{8,0},{9,1},... | collective-permute-start | bytes 294920 | tf_op jit(solution)/shard_map/ppermute | solution.py:60
  37.1 5.5 %collective-permute-done.5.refs_2_ = bf16[6,64,128]{2,1,0:T(8,128)(2,1)S(1)} collective-permute-done((bf16[6,64,128]{2,1,0:T(8,128)(2,1)S(1)}, bf16[6,64,128]{2,1,0:T(8,128)(2,1)S(1)}, u32[]{:S(2)}, u32[]{:S(2)}) %collective-permute-start.5) | collective-permute-done | bytes 98336 | tf_op jit(solution)/shard_map/ppermute | solution.py:60
  42.7 1.6 %collective-permute-start.7 = (bf16[6,64,128]{2,1,0:T(8,128)(2,1)S(1)}, bf16[6,64,128]{2,1,0:T(8,128)(2,1)S(1)}, u32[]{:S(2)}, u32[]{:S(2)}) collective-permute-start(bf16[6,64,128]{2,1,0:T(8,128)(2,1)S(1)} %shard_map.131.refs_0_), channel_id=1, source_target_pairs={{0,16},{1,17},{2,18},{3,19},{4,20},{5,21},{6,22},{7,23},{8,24},{9,... | collective-permute-start | bytes 294920 | tf_op jit(solution)/shard_map/ppermute | solution.py:60
  44.3 0.6 fusion.1
  44.9 2.5 %collective-permute-done.7.refs_1_ = bf16[6,64,128]{2,1,0:T(8,128)(2,1)S(1)} collective-permute-done((bf16[6,64,128]{2,1,0:T(8,128)(2,1)S(1)}, bf16[6,64,128]{2,1,0:T(8,128)(2,1)S(1)}, u32[]{:S(2)}, u32[]{:S(2)}) %collective-permute-start.7) | collective-permute-done | bytes 98336 | tf_op jit(solution)/shard_map/ppermute | solution.py:60
  47.4 5.6 %shard_map.133 = (bf16[6,128,128]{2,1,0:T(8,128)(2,1)S(1)}, f32[6,128,128]{2,1,0:T(8,128)}, bf16[6,64,128]{2,1,0:T(8,128)(2,1)S(1)}) custom-call(s32[4]{0:T(128)S(1)} %pad_add_fusion.place, s32[1]{0:T(128)} %bitcast.4.held, f32[1]{0:T(128)S(6)} %sub.12.correction, bf16[6,64,128]{2,1,0:T(8,128)(2,1)S(1)} %shard_map.131.refs_0_, ...), custom_call_target="tpu_custom_call" | custom-call | flops 276824064 | bytes 2850816 | tf_op jit(solution)/shard_map/pallas_call | solution.py:25
  53.0 2.5 %collective-permute-start.10 = (bf16[6,64,128]{2,1,0:T(8,128)(2,1)S(1)}, bf16[6,64,128]{2,1,0:T(8,128)(2,1)S(1)}, u32[]{:S(2)}, u32[]{:S(2)}) collective-permute-start(bf16[6,64,128]{2,1,0:T(8,128)(2,1)S(1)} %get-tuple-element.23.refs_0_), channel_id=1, source_target_pairs={{0,12},{1,13},{2,14},{3,15},{4,8},{5,9},{6,10},{7,11},{8,4},{9,5},... | collective-permute-start | bytes 294920 | tf_op jit(solution)/shard_map/ppermute | solution.py:60
  55.5 0.7 collective-permute-start.8
  56.2 1.2 %collective-permute-start.9 = (bf16[6,64,128]{2,1,0:T(8,128)(2,1)S(1)}, bf16[6,64,128]{2,1,0:T(8,128)(2,1)S(1)}, u32[]{:S(2)}, u32[]{:S(2)}) collective-permute-start(bf16[6,64,128]{2,1,0:T(8,128)(2,1)S(1)} %get-tuple-element.23.refs_0_), channel_id=1, source_target_pairs={{0,8},{1,9},{2,10},{3,11},{4,12},{5,13},{6,14},{7,15},{8,0},{9,1},... | collective-permute-start | bytes 294920 | tf_op jit(solution)/shard_map/ppermute | solution.py:60
  57.4 2.2 %collective-permute-done.10.refs_3_ = bf16[6,64,128]{2,1,0:T(8,128)(2,1)S(1)} collective-permute-done((bf16[6,64,128]{2,1,0:T(8,128)(2,1)S(1)}, bf16[6,64,128]{2,1,0:T(8,128)(2,1)S(1)}, u32[]{:S(2)}, u32[]{:S(2)}) %collective-permute-start.10) | collective-permute-done | bytes 98336 | tf_op jit(solution)/shard_map/ppermute | solution.py:60
  59.6 1.1 %collective-permute-done.8.refs_1_ = bf16[6,64,128]{2,1,0:T(8,128)(2,1)S(1)} collective-permute-done((bf16[6,64,128]{2,1,0:T(8,128)(2,1)S(1)}, bf16[6,64,128]{2,1,0:T(8,128)(2,1)S(1)}, u32[]{:S(2)}, u32[]{:S(2)}) %collective-permute-start.8) | collective-permute-done | bytes 98336 | tf_op jit(solution)/shard_map/ppermute | solution.py:60
  60.7 2.1 %collective-permute-done.9.refs_2_ = bf16[6,64,128]{2,1,0:T(8,128)(2,1)S(1)} collective-permute-done((bf16[6,64,128]{2,1,0:T(8,128)(2,1)S(1)}, bf16[6,64,128]{2,1,0:T(8,128)(2,1)S(1)}, u32[]{:S(2)}, u32[]{:S(2)}) %collective-permute-start.9) | collective-permute-done | bytes 98336 | tf_op jit(solution)/shard_map/ppermute | solution.py:60
  63.3 1.6 %collective-permute-start.11 = (bf16[24,64,128]{2,1,0:T(8,128)(2,1)S(1)}, bf16[24,64,128]{2,1,0:T(8,128)(2,1)S(1)}, u32[]{:S(2)}, u32[]{:S(2)}) collective-permute-start(bf16[24,64,128]{2,1,0:T(8,128)(2,1)S(1)} %shard_map.134.refs_0_), channel_id=1, source_target_pairs={{0,16},{1,17},{2,18},{3,19},{4,20},{5,21},{6,22},{7,23},{8,24},{9,... | collective-permute-start | bytes 1179656 | tf_op jit(solution)/shard_map/ppermute | solution.py:60
  64.9 1.5 %collective-permute-start.12 = (bf16[24,64,128]{2,1,0:T(8,128)(2,1)S(1)}, bf16[24,64,128]{2,1,0:T(8,128)(2,1)S(1)}, u32[]{:S(2)}, u32[]{:S(2)}) collective-permute-start(bf16[24,64,128]{2,1,0:T(8,128)(2,1)S(1)} %shard_map.134.refs_0_), channel_id=1, source_target_pairs={{0,2},{1,3},{2,0},{3,1},{4,6},{5,7},{6,4},{7,5},{8,10},{9,11},{10,... | collective-permute-start | bytes 1179656 | tf_op jit(solution)/shard_map/ppermute | solution.py:60
  66.9 7.7 %collective-permute-done.11.refs_1_ = bf16[24,64,128]{2,1,0:T(8,128)(2,1)S(1)} collective-permute-done((bf16[24,64,128]{2,1,0:T(8,128)(2,1)S(1)}, bf16[24,64,128]{2,1,0:T(8,128)(2,1)S(1)}, u32[]{:S(2)}, u32[]{:S(2)}) %collective-permute-start.11) | collective-permute-done | bytes 393248 | tf_op jit(solution)/shard_map/ppermute | solution.py:60
  74.6 2.1 %collective-permute-done.12.refs_2_ = bf16[24,64,128]{2,1,0:T(8,128)(2,1)S(1)} collective-permute-done((bf16[24,64,128]{2,1,0:T(8,128)(2,1)S(1)}, bf16[24,64,128]{2,1,0:T(8,128)(2,1)S(1)}, u32[]{:S(2)}, u32[]{:S(2)}) %collective-permute-start.12) | collective-permute-done | bytes 393248 | tf_op jit(solution)/shard_map/ppermute | solution.py:60
  76.7 4.2 %collective-permute-done.13.refs_3_ = bf16[24,64,128]{2,1,0:T(8,128)(2,1)S(1)} collective-permute-done((bf16[24,64,128]{2,1,0:T(8,128)(2,1)S(1)}, bf16[24,64,128]{2,1,0:T(8,128)(2,1)S(1)}, u32[]{:S(2)}, u32[]{:S(2)}) %collective-permute-start.13) | collective-permute-done | bytes 393248 | tf_op jit(solution)/shard_map/ppermute | solution.py:60
  80.9 6.5 %shard_map.136 = f32[6,128,128]{2,1,0:T(8,128)} custom-call(s32[1]{0:T(128)} %bitcast.4.held, bf16[6,128,128]{2,1,0:T(8,128)(2,1)S(1)} %get-tuple-element.25.gradient, f32[6,128,128]{2,1,0:T(8,128)S(1)} %copy-done.8, f32[6,128,128]{2,1,0:T(8,128)S(1)} %copy-done.1), custom_call_target="tpu_custom_call" | custom-call | flops 1006632960 | bytes 1376256 | tf_op jit(solution)/shard_map/pallas_call | solution.py:25
  87.4 6.4 %shard_map.137 = f32[6,128,128]{2,1,0:T(8,128)} custom-call(s32[1]{0:T(128)} %bitcast.4.held, bf16[6,128,128]{2,1,0:T(8,128)(2,1)S(1)} %get-tuple-element.25.gradient, f32[6,128,128]{2,1,0:T(8,128)S(1)} %copy-done.9, f32[6,128,128]{2,1,0:T(8,128)S(1)} %copy-done.2), custom_call_target="tpu_custom_call" | custom-call | flops 1006632960 | bytes 1376256 | tf_op jit(solution)/shard_map/pallas_call | solution.py:25
  93.8 4.0 %shard_map.135 = bf16[48,128,128]{2,1,0:T(8,128)(2,1)} custom-call(s32[4]{0:T(128)S(1)} %pad_add_fusion.place, s32[48]{0:T(128)S(1)} %copy-done.7, s32[48]{0:T(128)S(1)} %convert_reduce_fusion.rank, bf16[24,64,128]{2,1,0:T(8,128)(2,1)S(1)} %shard_map.134.refs_0_, bf16[24,64,128]{2,1,0:T(8,128)(2,1)S(1)} %collective-permute-done.11.refs_1_, ...), custom_call_target="tpu_custom_call" | custom-call | bytes 4718592 | tf_op jit(solution)/shard_map/pallas_call | solution.py:25
  (36 shorter events, 2.5 us)
Async XLA Ops:
  0.6 3.8 %collective-permute-start = (bf16[48,128,128]{2,1,0:T(8,128)(2,1)}, bf16[48,128,128]{2,1,0:T(8,128)(2,1)S(1)}, u32[]{:S(2)}, u32[]{:S(2)}) collective-permute-start(bf16[48,128,128]{2,1,0:T(8,128)(2,1)} %bitcast.6), channel_id=1, source_target_pairs={{0,1},{1,0},{2,3},{3,2},{4,5},{5,4},{6,7},{7,6},{8,9},{9,8},{10,11... | collective-permute-start | bytes 4718600 | tf_op jit(solution)/shard_map/ppermute | solution.py:60
  4.4 1.4 %copy-start = (bf16[1,48,128,128]{3,2,1,0:T(8,128)(2,1)S(1)}, bf16[1,48,128,128]{3,2,1,0:T(8,128)(2,1)}, u32[]{:S(2)}) copy-start(bf16[1,48,128,128]{3,2,1,0:T(8,128)(2,1)} %param.10) | copy-start | bytes 4718596
  5.8 0.7 copy-start.6
  8.5 28.0 %copy-start.1 = (f32[6,128,128]{2,1,0:T(8,128)S(1)}, f32[6,128,128]{2,1,0:T(8,128)}, u32[]{:S(2)}) copy-start(f32[6,128,128]{2,1,0:T(8,128)} %basis.2) | copy-start | bytes 1179652
  8.5 27.9 %copy-start.2 = (f32[6,128,128]{2,1,0:T(8,128)S(1)}, f32[6,128,128]{2,1,0:T(8,128)}, u32[]{:S(2)}) copy-start(f32[6,128,128]{2,1,0:T(8,128)} %basis.3) | copy-start | bytes 1179652
  8.5 27.9 %copy-start.3 = (f32[6,128,128]{2,1,0:T(8,128)S(1)}, f32[6,128,128]{2,1,0:T(8,128)}, u32[]{:S(2)}) copy-start(f32[6,128,128]{2,1,0:T(8,128)} %moment.1) | copy-start | bytes 1179652
  8.5 12.3 %collective-permute-start.1 = (bf16[24,64,128]{2,1,0:T(8,128)(2,1)S(1)}, bf16[24,64,128]{2,1,0:T(8,128)(2,1)S(1)}, u32[]{:S(2)}, u32[]{:S(2)}) collective-permute-start(bf16[24,64,128]{2,1,0:T(8,128)(2,1)S(1)} %get-tuple-element.16), channel_id=1, source_target_pairs={{0,16},{1,17},{2,18},{3,19},{4,20},{5,21},{6,22},{7,23},{8,24},{9,... | collective-permute-start | bytes 1179656 | tf_op jit(solution)/shard_map/ppermute | solution.py:60
  11.5 12.0 %collective-permute-start.2 = (bf16[24,64,128]{2,1,0:T(8,128)(2,1)S(1)}, bf16[24,64,128]{2,1,0:T(8,128)(2,1)S(1)}, u32[]{:S(2)}, u32[]{:S(2)}) collective-permute-start(bf16[24,64,128]{2,1,0:T(8,128)(2,1)S(1)} %get-tuple-element.17), channel_id=1, source_target_pairs={{0,2},{1,3},{2,0},{3,1},{4,6},{5,7},{6,4},{7,5},{8,10},{9,11},{10,... | collective-permute-start | bytes 1179656 | tf_op jit(solution)/shard_map/ppermute | solution.py:60
  13.0 17.6 %collective-permute-start.3 = (bf16[24,64,128]{2,1,0:T(8,128)(2,1)S(1)}, bf16[24,64,128]{2,1,0:T(8,128)(2,1)S(1)}, u32[]{:S(2)}, u32[]{:S(2)}) collective-permute-start(bf16[24,64,128]{2,1,0:T(8,128)(2,1)S(1)} %get-tuple-element.18), channel_id=1, source_target_pairs={{0,18},{1,19},{2,16},{3,17},{4,22},{5,23},{6,20},{7,21},{8,26},{9,... | collective-permute-start | bytes 1179656 | tf_op jit(solution)/shard_map/ppermute | solution.py:60
  30.6 13.7 %copy-start.7 = (s32[48]{0:T(128)S(1)}, s32[48]{0:T(128)}, u32[]{:S(2)}) copy-start(s32[48]{0:T(128)} %owners.3) | copy-start | bytes 580
  30.6 16.8 %copy-start.4 = (f32[6,128,128]{2,1,0:T(8,128)S(1)}, f32[6,128,128]{2,1,0:T(8,128)}, u32[]{:S(2)}) copy-start(f32[6,128,128]{2,1,0:T(8,128)} %refs_3_.1) | copy-start | bytes 1179652
  30.6 16.8 %copy-start.5 = (f32[6,128,128]{2,1,0:T(8,128)S(1)}, f32[6,128,128]{2,1,0:T(8,128)}, u32[]{:S(2)}) copy-start(f32[6,128,128]{2,1,0:T(8,128)} %refs_4_.1) | copy-start | bytes 1179652
  31.3 5.8 %collective-permute-start.4 = (bf16[6,64,128]{2,1,0:T(8,128)(2,1)S(1)}, bf16[6,64,128]{2,1,0:T(8,128)(2,1)S(1)}, u32[]{:S(2)}, u32[]{:S(2)}) collective-permute-start(bf16[6,64,128]{2,1,0:T(8,128)(2,1)S(1)} %get-tuple-element.20), channel_id=1, source_target_pairs={{0,4},{1,5},{2,6},{3,7},{4,0},{5,1},{6,2},{7,3},{8,12},{9,13},{10,... | collective-permute-start | bytes 294920 | tf_op jit(solution)/shard_map/ppermute | solution.py:60
  33.1 9.5 %collective-permute-start.5 = (bf16[6,64,128]{2,1,0:T(8,128)(2,1)S(1)}, bf16[6,64,128]{2,1,0:T(8,128)(2,1)S(1)}, u32[]{:S(2)}, u32[]{:S(2)}) collective-permute-start(bf16[6,64,128]{2,1,0:T(8,128)(2,1)S(1)} %get-tuple-element.21), channel_id=1, source_target_pairs={{0,8},{1,9},{2,10},{3,11},{4,12},{5,13},{6,14},{7,15},{8,0},{9,1},... | collective-permute-start | bytes 294920 | tf_op jit(solution)/shard_map/ppermute | solution.py:60
  35.7 6.9 %collective-permute-start.6 = (bf16[6,64,128]{2,1,0:T(8,128)(2,1)S(1)}, bf16[6,64,128]{2,1,0:T(8,128)(2,1)S(1)}, u32[]{:S(2)}, u32[]{:S(2)}) collective-permute-start(bf16[6,64,128]{2,1,0:T(8,128)(2,1)S(1)} %get-tuple-element.22), channel_id=1, source_target_pairs={{0,12},{1,13},{2,14},{3,15},{4,8},{5,9},{6,10},{7,11},{8,4},{9,5},... | collective-permute-start | bytes 294920 | tf_op jit(solution)/shard_map/ppermute | solution.py:60
  42.7 38.2 %copy-start.8 = (f32[6,128,128]{2,1,0:T(8,128)S(1)}, f32[6,128,128]{2,1,0:T(8,128)}, u32[]{:S(2)}) copy-start(f32[6,128,128]{2,1,0:T(8,128)} %stat.2) | copy-start | bytes 1179652
  42.7 4.7 %collective-permute-start.7 = (bf16[6,64,128]{2,1,0:T(8,128)(2,1)S(1)}, bf16[6,64,128]{2,1,0:T(8,128)(2,1)S(1)}, u32[]{:S(2)}, u32[]{:S(2)}) collective-permute-start(bf16[6,64,128]{2,1,0:T(8,128)(2,1)S(1)} %shard_map.131.refs_0_), channel_id=1, source_target_pairs={{0,16},{1,17},{2,18},{3,19},{4,20},{5,21},{6,22},{7,23},{8,24},{9,... | collective-permute-start | bytes 294920 | tf_op jit(solution)/shard_map/ppermute | solution.py:60
  53.0 6.6 %collective-permute-start.10 = (bf16[6,64,128]{2,1,0:T(8,128)(2,1)S(1)}, bf16[6,64,128]{2,1,0:T(8,128)(2,1)S(1)}, u32[]{:S(2)}, u32[]{:S(2)}) collective-permute-start(bf16[6,64,128]{2,1,0:T(8,128)(2,1)S(1)} %get-tuple-element.23.refs_0_), channel_id=1, source_target_pairs={{0,12},{1,13},{2,14},{3,15},{4,8},{5,9},{6,10},{7,11},{8,4},{9,5},... | collective-permute-start | bytes 294920 | tf_op jit(solution)/shard_map/ppermute | solution.py:60
  55.5 5.2 %collective-permute-start.8 = (bf16[6,64,128]{2,1,0:T(8,128)(2,1)S(1)}, bf16[6,64,128]{2,1,0:T(8,128)(2,1)S(1)}, u32[]{:S(2)}, u32[]{:S(2)}) collective-permute-start(bf16[6,64,128]{2,1,0:T(8,128)(2,1)S(1)} %get-tuple-element.23.refs_0_), channel_id=1, source_target_pairs={{0,4},{1,5},{2,6},{3,7},{4,0},{5,1},{6,2},{7,3},{8,12},{9,13},{10,... | collective-permute-start | bytes 294920 | tf_op jit(solution)/shard_map/ppermute | solution.py:60
  56.2 6.6 %collective-permute-start.9 = (bf16[6,64,128]{2,1,0:T(8,128)(2,1)S(1)}, bf16[6,64,128]{2,1,0:T(8,128)(2,1)S(1)}, u32[]{:S(2)}, u32[]{:S(2)}) collective-permute-start(bf16[6,64,128]{2,1,0:T(8,128)(2,1)S(1)} %get-tuple-element.23.refs_0_), channel_id=1, source_target_pairs={{0,8},{1,9},{2,10},{3,11},{4,12},{5,13},{6,14},{7,15},{8,0},{9,1},... | collective-permute-start | bytes 294920 | tf_op jit(solution)/shard_map/ppermute | solution.py:60
  63.3 11.2 %collective-permute-start.11 = (bf16[24,64,128]{2,1,0:T(8,128)(2,1)S(1)}, bf16[24,64,128]{2,1,0:T(8,128)(2,1)S(1)}, u32[]{:S(2)}, u32[]{:S(2)}) collective-permute-start(bf16[24,64,128]{2,1,0:T(8,128)(2,1)S(1)} %shard_map.134.refs_0_), channel_id=1, source_target_pairs={{0,16},{1,17},{2,18},{3,19},{4,20},{5,21},{6,22},{7,23},{8,24},{9,... | collective-permute-start | bytes 1179656 | tf_op jit(solution)/shard_map/ppermute | solution.py:60
  64.9 11.8 %collective-permute-start.12 = (bf16[24,64,128]{2,1,0:T(8,128)(2,1)S(1)}, bf16[24,64,128]{2,1,0:T(8,128)(2,1)S(1)}, u32[]{:S(2)}, u32[]{:S(2)}) collective-permute-start(bf16[24,64,128]{2,1,0:T(8,128)(2,1)S(1)} %shard_map.134.refs_0_), channel_id=1, source_target_pairs={{0,2},{1,3},{2,0},{3,1},{4,6},{5,7},{6,4},{7,5},{8,10},{9,11},{10,... | collective-permute-start | bytes 1179656 | tf_op jit(solution)/shard_map/ppermute | solution.py:60
  66.4 14.4 %collective-permute-start.13 = (bf16[24,64,128]{2,1,0:T(8,128)(2,1)S(1)}, bf16[24,64,128]{2,1,0:T(8,128)(2,1)S(1)}, u32[]{:S(2)}, u32[]{:S(2)}) collective-permute-start(bf16[24,64,128]{2,1,0:T(8,128)(2,1)S(1)} %shard_map.134.refs_0_), channel_id=1, source_target_pairs={{0,18},{1,19},{2,16},{3,17},{4,22},{5,23},{6,20},{7,21},{8,26},{9,... | collective-permute-start | bytes 1179656 | tf_op jit(solution)/shard_map/ppermute | solution.py:60
  66.9 26.8 %collective-permute-start.14 = (bf16[24,64,128]{2,1,0:T(8,128)(2,1)S(1)}, bf16[24,64,128]{2,1,0:T(8,128)(2,1)S(1)}, u32[]{:S(2)}, u32[]{:S(2)}) collective-permute-start(bf16[24,64,128]{2,1,0:T(8,128)(2,1)S(1)} %shard_map.134.refs_0_), channel_id=1, source_target_pairs={{0,1},{1,0},{2,3},{3,2},{4,5},{5,4},{6,7},{7,6},{8,9},{9,8},{10,11... | collective-permute-start | bytes 1179656 | tf_op jit(solution)/shard_map/ppermute | solution.py:60
  74.6 19.2 %collective-permute-start.15 = (bf16[24,64,128]{2,1,0:T(8,128)(2,1)S(1)}, bf16[24,64,128]{2,1,0:T(8,128)(2,1)S(1)}, u32[]{:S(2)}, u32[]{:S(2)}) collective-permute-start(bf16[24,64,128]{2,1,0:T(8,128)(2,1)S(1)} %collective-permute-done.11.refs_1_), channel_id=1, source_target_pairs={{0,1},{1,0},{2,3},{3,2},{4,5},{5,4},{6,7},{7,6},{8,9},{9,8},{10,11... | collective-permute-start | bytes 1179656 | tf_op jit(solution)/shard_map/ppermute | solution.py:60
  76.7 17.0 %collective-permute-start.16 = (bf16[24,64,128]{2,1,0:T(8,128)(2,1)S(1)}, bf16[24,64,128]{2,1,0:T(8,128)(2,1)S(1)}, u32[]{:S(2)}, u32[]{:S(2)}) collective-permute-start(bf16[24,64,128]{2,1,0:T(8,128)(2,1)S(1)} %collective-permute-done.12.refs_2_), channel_id=1, source_target_pairs={{0,1},{1,0},{2,3},{3,2},{4,5},{5,4},{6,7},{7,6},{8,9},{9,8},{10,11... | collective-permute-start | bytes 1179656 | tf_op jit(solution)/shard_map/ppermute | solution.py:60
  80.9 12.9 %collective-permute-start.17 = (bf16[24,64,128]{2,1,0:T(8,128)(2,1)S(1)}, bf16[24,64,128]{2,1,0:T(8,128)(2,1)S(1)}, u32[]{:S(2)}, u32[]{:S(2)}) collective-permute-start(bf16[24,64,128]{2,1,0:T(8,128)(2,1)S(1)} %collective-permute-done.13.refs_3_), channel_id=1, source_target_pairs={{0,1},{1,0},{2,3},{3,2},{4,5},{5,4},{6,7},{7,6},{8,9},{9,8},{10,11... | collective-permute-start | bytes 1179656 | tf_op jit(solution)/shard_map/ppermute | solution.py:60
  80.9 6.5 %copy-start.9 = (f32[6,128,128]{2,1,0:T(8,128)S(1)}, f32[6,128,128]{2,1,0:T(8,128)}, u32[]{:S(2)}) copy-start(f32[6,128,128]{2,1,0:T(8,128)} %stat.3) | copy-start | bytes 1179652

commit v2 on v0

v2 whole, which is shorter than its diff:
```python
import functools
import math

import jax
import jax.numpy as jnp
from jax import lax
from jax.experimental import pallas as pl
from jax.experimental.pallas import tpu as pltpu
from jax.sharding import PartitionSpec as P

NS_ITERS = 6
AXES = ("dp", "owner")
F32 = jnp.float32
BF16 = jnp.bfloat16
VMEM_LIMIT = 48 * 1024 * 1024
VMEM = pl.BlockSpec(memory_space=pltpu.VMEM)
SMEM = pl.BlockSpec(memory_space=pltpu.SMEM)
HBM = pl.BlockSpec(memory_space=pltpu.HBM)


def shape(dims, dtype):
    return jax.ShapeDtypeStruct(dims, dtype)


class Chain:
    def __init__(self):
        self.token = None

    def call(self, kernel, scalars, arrays, outs, flops=0, scratch=(), specs=None, moved=0):
        moved = moved or sum(a.size * a.dtype.itemsize for a in list(arrays) + list(outs))
        count = len(scalars) + len(arrays)
        tokens = () if self.token is None else (self.token,)
        specs = specs or [VMEM] * len(outs)

        def run(*refs):
            refs = list(refs)
            token = refs.pop(count + len(tokens) + len(outs))
            kernel(*refs[:count], *refs[count + len(tokens) :])
            token[...] = jnp.zeros_like(token)

        *results, self.token = pl.pallas_call(
            run,
            out_shape=(*outs, shape((8, 128), F32)),
            in_specs=[SMEM] * len(scalars)
            + [VMEM] * len(arrays)
            + [VMEM] * len(tokens),
            out_specs=(*specs, VMEM),
            scratch_shapes=list(scratch),
            compiler_params=pltpu.CompilerParams(vmem_limit_bytes=VMEM_LIMIT),
            cost_estimate=pl.CostEstimate(flops=flops, bytes_accessed=moved, transcendentals=0),
        )(*scalars, *arrays, *tokens)
        return results


class Grid:
    def __init__(self, dp_count, owner_count):
        self.dp, self.core = dp_count, 2
        self.high = 4
        self.middle = owner_count // (self.core * self.high)
        self.owners = owner_count

    def place(self):
        owner = lax.axis_index("owner")
        return jnp.stack(
            [
                lax.axis_index("dp"),
                owner // (self.core * self.middle),
                owner // self.core % self.middle,
                owner % self.core,
            ]
        ).astype(jnp.int32)

    def swap(self, array, dp=0, high=0, middle=0, core=0):
        step = (high * self.middle + middle) * self.core + core
        pairs = [
            (d * self.owners + o, (d ^ dp) * self.owners + (o ^ step))
            for d in range(self.dp)
            for o in range(self.owners)
        ]
        return lax.ppermute(array, AXES, pairs)


def split(value):
    top = value.astype(BF16)
    return top, (value - top.astype(F32)).astype(BF16)


def dot(left, right, dims):
    return lax.dot_general(left, right, (dims, ((), ())), preferred_element_type=F32)


NN = ((1,), (0,))
NT = ((1,), (1,))
TN = ((0,), (0,))


def as_left(value, axis=1):
    return jnp.concatenate(split(value), axis)


def as_right(value):
    half = jnp.concatenate(split(value), 1)
    return jnp.concatenate([half, half], 0)


def product(left, right, dims=NN):
    wide = dot(left, right, dims)
    size = wide.shape[1] // 2
    return wide[:, :size] + wide[:, size:]


def log2(count):
    return count.bit_length() - 1


class Table:
    def __init__(self, grid, slots):
        self.columns = grid.middle * grid.core
        self.groups = math.gcd(slots, grid.dp)
        self.shares = grid.dp // self.groups
        self.each = slots // self.groups
        self.length = grid.high * self.each
        self.rooms = (self.length * 2 // 3, self.length * 3 // 4, self.length)
        self.listed = 0
        self.counts = self.columns * self.groups * self.length
        self.inverse = self.counts + self.columns * self.groups
        self.held = self.inverse + self.length
        self.place = self.held + 1
        self.size = self.place + 4

    def slot(self, info, group, index):
        turn = group + self.groups - lax.rem(info[self.place + 1], self.groups)
        return self.groups * index + lax.rem(turn, self.groups)


def table_kernel(grid, table, place, owners, out, level, seen):
    for owner in range(grid.owners):
        seen[owner] = 0
    for part in range(table.columns * table.groups):
        out[table.counts + part] = 0
    for at in range(table.length):
        out[table.inverse + at] = -1
    column_mine = place[2] * grid.core + place[3]
    mine = column_mine * table.groups + lax.div(place[0], table.shares)

    def step(block, carry):
        owner = owners[block]
        rank = seen[owner]
        seen[owner] = rank + 1
        column, high = owner & (table.columns - 1), owner >> log2(table.columns)
        group, index = (rank + high) & (table.groups - 1), rank >> log2(table.groups)
        part = column * table.groups + group
        at = out[table.counts + part]
        out[table.counts + part] = at + 1
        out[table.listed + part * table.length + at] = block

        @pl.when(part == mine)
        def _():
            out[table.inverse + high * table.each + index] = at

        return carry

    lax.fori_loop(0, owners.shape[0], step, 0, unroll=8)
    out[table.held] = seen[place[1] * table.columns + column_mine]
    most = out[table.counts]
    for part in range(1, table.columns * table.groups):
        most = jnp.maximum(most, out[table.counts + part])
    level[0] = sum((most > room).astype(jnp.int32) for room in table.rooms[:-1])
    for at in range(4):
        out[table.place + at] = place[at]


def part_of(grid, table, info, dc, dm, dd):
    column = (info[table.place + 2] ^ dm) * grid.core + (info[table.place + 3] ^ dc)
    dp = info[table.place] ^ dd
    part = column * table.groups + lax.div(dp, table.shares)
    return info[table.counts + part], table.listed + part * table.length, lax.rem(dp, table.shares)


def copy_kernel(source, out):
    out[...] = source[...]


def spread_kernel(grid, table, info, own, other, *outs):
    rows = own.shape[1] // table.shares
    for dm in range(grid.middle):
        for dd in range(grid.dp):
            count, first, share = part_of(grid, table, info, 0, dm, dd)
            part = pl.ds(pl.multiple_of(share * rows, rows), rows)

            def put(out, at, carry):
                block = info[first + at]
                total = own[block, part].astype(F32) + other[block, part].astype(F32)
                out[at] = total.astype(BF16)
                return carry

            lax.fori_loop(0, count, functools.partial(put, outs[dm * grid.dp + dd]), 0)


def total_of(arrays, at):
    total = arrays[0][at].astype(F32)
    for array in arrays[1:]:
        total = total + array[at].astype(F32)
    return total.astype(BF16)


def gather_sum_kernel(grid, table, info, *refs):
    count = grid.middle * grid.dp
    arrays, outs = refs[:count], refs[count:]
    for dh in range(grid.high):
        first = table.inverse + (info[table.place + 1] ^ dh) * table.each
        for index in range(table.each):
            at = jnp.clip(info[first + index], 0, arrays[0].shape[0] - 1)
            outs[dh][index] = total_of(arrays, at)


def sum_kernel(*refs):
    arrays, out = refs[:-1], refs[-1]
    for slot in range(out.shape[0]):
        out[slot] = total_of(arrays, slot)


def prepare_kernel(moment, left, right, rot_old, left_plain, left_turned, right_tall, right_turned):
    for slot in range(rot_old.shape[0]):
        left_t, right_t = left[slot].T, right[slot].T
        half = product(as_left(moment[slot]), as_right(right[slot]))
        left_turned[slot] = as_left(left_t)
        rot_old[slot] = product(as_left(left_t), as_right(half))
        left_plain[slot] = as_left(left[slot])
        right_tall[slot] = as_left(right[slot], 0)
        right_turned[slot] = as_right(right_t)


def rotate(gradient, rot_old, second, left_turned, right_tall, right_turned, c, pairs):
    halves = [dot(jnp.concatenate([gradient[i]] * 2, 1), right_tall[slot], NN) for i, slot in pairs]
    rotated = [
        product(left_turned[slot], as_right(half)) for half, (_, slot) in zip(halves, pairs, strict=True)
    ]
    turned = []
    for value, (_, slot) in zip(rotated, pairs, strict=True):
        rot_moment = 0.95 * rot_old[slot] + 0.05 * value
        second_new = 0.95 * second[slot] + 0.05 * value * value
        scaled = rot_moment / c / (jnp.sqrt(second_new / c) + 1e-08)
        turned.append(product(as_left(scaled), right_turned[slot]))
    return turned


def step_kernel(grid, table, info, correction, *refs):
    parts = refs[: table.shares]
    (rot_old, second, master, left_plain, left_turned, right_tall, right_turned) = refs[table.shares : -2]
    gradient, updated = refs[-2:]
    rows = parts[0].shape[1]
    dp = info[table.place]
    group, share = lax.div(dp, table.shares), lax.rem(dp, table.shares)
    for dd in range(table.shares):
        gradient[:, pl.ds(pl.multiple_of((share ^ dd) * rows, rows), rows), :] = parts[dd][...]
    mine = pl.ds(pl.multiple_of(share * rows, rows), rows)
    pairs = [(index, table.slot(info, group, index)) for index in range(table.each)]
    turned = rotate(
        gradient, rot_old, second, left_turned, right_tall, right_turned, correction[0], pairs
    )
    for value, (index, slot) in zip(turned, pairs, strict=True):
        weights = master[slot, mine]
        moved = product(left_plain[slot, mine], as_right(value))
        moved = jnp.where(slot < info[table.held], moved, 0.0)
        updated[index] = (weights - 0.01 * (moved + 0.1 * weights)).astype(BF16)


def direction_kernel(table, info, correction, *refs):
    gradients = refs[: table.groups]
    (rot_old, second, left_plain, left_turned, right_tall, right_turned, direction) = refs[table.groups :]
    group = lax.div(info[table.place], table.shares)
    for dg, gradient in enumerate(gradients):
        pairs = [(index, table.slot(info, group ^ dg, index)) for index in range(table.each)]
        turned = rotate(
            gradient, rot_old, second, left_turned, right_tall, right_turned, correction[0], pairs
        )
        for value, (_, slot) in zip(turned, pairs, strict=True):
            moved = product(left_plain[slot], as_right(value))
            direction[slot] = jnp.where(slot < info[table.held], moved, 0.0)


def refresh(gradient, left_stat, right_stat, left, right, pairs):
    iterates = []
    for dims, stat, basis in ((NT, left_stat, left), (TN, right_stat, right)):
        for index, slot in pairs:
            gram = dot(gradient[index], gradient[index], dims)
            power = product(as_left(0.95 * stat[slot] + 0.05 * gram), as_right(basis[slot]))
            iterates.append(power / (jnp.sqrt(jnp.sum(power * power)) + 1e-06))
    for _ in range(NS_ITERS):
        squares = [product(as_left(x, 0), as_right(x), TN) for x in iterates]
        iterates = [
            1.5 * x - 0.5 * product(as_left(x), as_right(square))
            for x, square in zip(iterates, squares, strict=True)
        ]
    return iterates[: len(pairs)], iterates[len(pairs) :]


def refresh_kernel(table, first, info, *refs):
    count = table.groups - 1 if first else 1
    gradients, (left_stat, right_stat, left, right) = refs[:count], refs[count : count + 4]
    done, (left_out, right_out) = refs[count + 4 : -2], refs[-2:]
    group = lax.div(info[table.place], table.shares)

    def put(slot, new_left, new_right):
        live = slot < info[table.held]
        left_out[slot] = jnp.where(live, new_left, left[slot])
        right_out[slot] = jnp.where(live, new_right, right[slot])

    for dg, gradient in enumerate(gradients, first):
        pairs = [(index, table.slot(info, group ^ dg, index)) for index in range(table.each)]
        new_left, new_right = refresh(gradient, left_stat, right_stat, left, right, pairs)
        for index, slot in pairs:
            if first:
                put(slot, new_left[index], new_right[index])
            else:
                left_out[index], right_out[index] = new_left[index], new_right[index]
    if first:
        for index in range(table.each):
            put(table.slot(info, group, index), done[0][index], done[1][index])


def join_kernel(grid, table, info, *refs):
    arrays, (out, every) = refs[: grid.high], refs[-2:]
    spare = info[table.counts + part_index(grid, table, info)]
    for dh in range(grid.high):
        first = table.inverse + (info[table.place + 1] ^ dh) * table.each
        for index in range(table.each):
            at = info[first + index]
            every[jnp.where(at < 0, spare, at)] = arrays[dh][index]
            spare = spare + (at < 0).astype(jnp.int32)
    out[...] = every[: out.shape[0]]


def part_index(grid, table, info):
    column = info[table.place + 2] * grid.core + info[table.place + 3]
    return column * table.groups + lax.div(info[table.place], table.shares)


def weights_kernel(grid, table, info, *refs):
    arrays, (out, sem) = refs[:-2], refs[-2:]
    rows = arrays[0].shape[1]
    sources = [(dc, dm, dd) for dc in range(grid.core) for dm in range(grid.middle) for dd in range(grid.dp)]
    for array, source in zip(arrays, sources, strict=True):
        count, first, share = part_of(grid, table, info, *source)
        part = pl.ds(pl.multiple_of(share * rows, rows), rows)

        def put(array, first, part, at, carry):
            pltpu.make_async_copy(array.at[at], out.at[info[first + at], part], sem).start()
            return carry

        lax.fori_loop(0, count, functools.partial(put, array, first, part), 0)
    pltpu.make_async_copy(out, out, sem).wait()


def body(
    partials,
    owners,
    step_count,
    master,
    moment,
    second,
    stat_left,
    stat_right,
    basis_left,
    basis_right,
):
    grid = Grid(lax.axis_size("dp"), lax.axis_size("owner"))
    table = Table(grid, master.shape[0])
    chain = Chain()
    correction = 1.0 - jnp.power(jnp.float32(0.95), step_count.astype(F32))
    own = partials[0]
    other = grid.swap(own, core=1)
    (fetched,) = chain.call(copy_kernel, (), (own,), [shape(own.shape, BF16)])
    info, level = chain.call(
        functools.partial(table_kernel, grid, table),
        (grid.place(), owners),
        (),
        [shape((table.size,), jnp.int32), shape((1,), jnp.int32)],
        scratch=(pltpu.SMEM((grid.owners,), jnp.int32),),
        specs=[SMEM, SMEM],
        moved=8 * 1024 * 1024,
    )
    states = (master, moment, second, stat_left, stat_right, basis_left, basis_right)
    return lax.switch(
        level[0],
        [functools.partial(update, grid, table, room) for room in table.rooms],
        chain.token,
        info,
        fetched,
        other,
        correction,
        *states,
    )


def update(
    grid,
    table,
    room,
    token,
    info,
    own,
    other,
    correction,
    master,
    moment,
    second,
    stat_left,
    stat_right,
    basis_left,
    basis_right,
):
    slots, size = master.shape[:2]
    blocks = own.shape[0]
    rows = size // table.shares
    chain = Chain()
    chain.token = token
    share = shape((table.each, rows, size), BF16)
    main = shape((room, rows, size), BF16)
    group_state = shape((table.each, size, size), F32)
    group_gradient = shape((table.each, size, size), BF16)
    state = shape((slots, size, size), F32)
    plane = [(dm, dd) for dm in range(grid.middle) for dd in range(grid.dp)]
    passes = slots * size**3

    def over_plane(arrays):
        order = sorted(range(1, len(plane)), key=lambda index: plane[index], reverse=True)
        got = {index: grid.swap(arrays[index], middle=plane[index][0], dp=plane[index][1]) for index in order}
        return [arrays[0]] + [got[index] for index in range(1, len(plane))]

    def over_high(arrays):
        return [arrays[0]] + [grid.swap(arrays[dh], high=dh) for dh in range(1, grid.high)]

    outs = chain.call(
        functools.partial(spread_kernel, grid, table), (info,), (own, other), [main] * len(plane)
    )
    got = over_plane(outs)
    rot_old, left_plain, left_turned, right_tall, right_turned = chain.call(
        prepare_kernel,
        (),
        (moment, basis_left, basis_right),
        [
            state,
            shape((slots, size, 2 * size), BF16),
            shape((slots, size, 2 * size), BF16),
            shape((slots, 2 * size, size), BF16),
            shape((slots, 2 * size, 2 * size), BF16),
        ],
        16 * passes,
    )
    outs = chain.call(
        functools.partial(gather_sum_kernel, grid, table), (info,), got, [share] * grid.high
    )
    (summed,) = chain.call(sum_kernel, (), over_high(outs), [share])
    parts = [summed] + [grid.swap(summed, dp=dd) for dd in range(1, table.shares)]
    gradient, updated = chain.call(
        functools.partial(step_kernel, grid, table),
        (info, correction),
        (*parts, rot_old, second, master, left_plain, left_turned, right_tall, right_turned),
        [group_gradient, share],
        14 * passes,
    )
    spread = over_high([updated] * grid.high)
    others = [grid.swap(gradient, dp=dg * table.shares) for dg in range(1, table.groups)]
    done = chain.call(
        functools.partial(refresh_kernel, table, 0),
        (info,),
        (gradient, stat_left, stat_right, basis_left, basis_right),
        [group_state, group_state],
        100 * passes,
    )
    (joined,) = chain.call(
        functools.partial(join_kernel, grid, table),
        (info,),
        (*spread, *others),
        [main],
        scratch=(pltpu.VMEM((table.length, rows, size), BF16),),
    )
    got = over_plane([joined] * len(plane))
    (direction,) = chain.call(
        functools.partial(direction_kernel, table),
        (info, correction),
        (gradient, *others, rot_old, second, left_plain, left_turned, right_tall, right_turned),
        [state],
        36 * passes,
    )
    left_new, right_new = chain.call(
        functools.partial(refresh_kernel, table, 1),
        (info,),
        (*others, stat_left, stat_right, basis_left, basis_right, *done),
        [state, state],
        100 * passes,
    )
    (got[-1],) = chain.call(copy_kernel, (), (got[-1],), [main])
    (weights_all,) = chain.call(
        functools.partial(weights_kernel, grid, table),
        (info,),
        (*got, *(grid.swap(a, core=1) for a in got)),
        [shape((blocks, size, size), BF16)],
        scratch=(pltpu.SemaphoreType.DMA,),
        specs=[HBM],
    )
    return (weights_all, direction, left_new, right_new)


def solution(mesh):
    placed = (
        P(("dp", "owner"), None, None, None),
        P(),
        P(),
        P("owner", None, None),
        P("owner", None, None),
        P("owner", None, None),
        P("owner", None, None),
        P("owner", None, None),
        P("owner", None, None),
        P("owner", None, None),
    )
    return jax.shard_map(
        body,
        mesh=mesh,
        in_specs=placed,
        out_specs=(P(), P("owner", None, None), P("owner", None, None), P("owner", None, None)),
        check_vma=False,
    )
```

time: 181 us -> 69.8 us (0.39)
  waiting for transfers between devices: 107 us -> 26.4 us
  matrix products: 31.2 us -> 0 us
  Pallas kernels: 0 us -> 19.3 us
  starting transfers between devices: 0.3 us -> 19.5 us
  local copies, waits for them, and re-layouts: 18.1 us -> 1.45 us
  between operations: 14.8 us -> 2.22 us
  other arithmetic: 8.79 us -> 0.08 us
    reduce_scatter x1 -> x0, waiting for transfers between devices: 62 us -> none  [body(): lax.psum_scatter(placed.astype(jnp.bfloat16), 'owner', scatter_dimension=...]
    dot_general x34 -> x0, matrix products: 31.2 us -> none  [product(): return jnp.matmul(left, right, precision=lax.Precision.HIGHEST)]
    ppermute x0 -> x18, waiting for transfers between devices: none -> 26.4 us  [swap(): return lax.ppermute(array, AXES, pairs)]
    psum x1 -> x0, waiting for transfers between devices: 23.2 us -> none  [body(): gradient = lax.psum(summed, 'dp').astype(jnp.float32)]
    all_gather x1 -> x0, waiting for transfers between devices: 21.6 us -> none  [body(): every_slot = lax.all_gather(updated, 'owner', axis=0, tiled=True)]
    ppermute x0 -> x18, starting transfers between devices: none -> 19.5 us  [swap(): return lax.ppermute(array, AXES, pairs)]
    pallas_call x0 -> x13, Pallas kernels: none -> 19.3 us  [call(): pl.pallas_call(run, out_shape=(*outs, shape((8, 128), F32)), in_specs=[SM...]
    gather x3 -> x0, local copies, waits for them, and re-layouts: 10.1 us -> none  [the longest x2 7.35 us: body(): placed = jnp.take(own_part, source, axis=0).astype(jnp.float32) * mask_all]
  transfers between devices with their start and end apart: 3 -> 18, of which waited for: 3 -> 10; matrix products, arithmetic and copies ran while one was open for 16% -> 0% of each run, Pallas kernels for 0% -> 19%
where the time goes in v2:
time: 69.8 us; the launch traced here: 69.6 us
  waiting for transfers between devices  26.4 us (38%)
  starting transfers between devices  19.5 us (28%)
  Pallas kernels  19.3 us (28%)
  between operations  2.22 us (3%)
  local copies, waits for them, and re-layouts  1.45 us (2%)
    ppermute x18, waiting for transfers between devices, swap(): return lax.ppermute(array, AXES, pairs)  26.4 us
    ppermute x18, starting transfers between devices, swap(): return lax.ppermute(array, AXES, pairs)  19.5 us
    pallas_call x13, Pallas kernels, call(): pl.pallas_call(run, out_shape=(*outs, shape((8, 128), F32)), in_specs=[SM...  19.3 us
    unnamed x6, local copies, waits for them, and re-layouts  1.42 us
  transfers between devices with their start and end apart: 18, of which 10 were waited for; matrix products, arithmetic and copies ran while one was open for 0% of the time, Pallas kernels for 19%

profile of v2, /device:TPU:0, one launch (start us, length us, event | category | flops | bytes accessed | tf_op | source)
XLA Modules:
  0.0 69.6 jit_solution(5011137052454529523)
XLA Ops:
  0.6 0.5 collective-permute-start.51
  1.2 1.4 %copy-done = bf16[1,48,128,128]{3,2,1,0:T(8,128)(2,1)S(1)} copy-done((bf16[1,48,128,128]{3,2,1,0:T(8,128)(2,1)S(1)}, bf16[1,48,128,128]{3,2,1,0:T(8,128)(2,1)}, u32[]{:S(2)}) %copy-start) | copy-done | bytes 1572888
  3.5 1.6 %shard_map.130 = (s32[121]{0:T(128)S(1)}, s32[1]{0:T(128)}, f32[8,128]{1,0:T(8,128)S(1)}) custom-call(s32[4]{0:T(128)S(1)} %pad_add_fusion.refs_0_, s32[48]{0:T(128)S(1)} %copy-done.1, f32[8,128]{1,0:T(8,128)S(1)} %get-tuple-element.219.refs_2_), custom_call_target="tpu_custom_call" | custom-call | bytes 8388608 | tf_op jit(solution)/shard_map/pallas_call | solution.py:41
  5.7 63.6 %conditional.1 = (bf16[48,128,128]{2,1,0:T(8,128)(2,1)}, f32[6,128,128]{2,1,0:T(8,128)}, f32[6,128,128]{2,1,0:T(8,128)}, f32[6,128,128]{2,1,0:T(8,128)}) conditional(s32[]{:T(128)} %bitcast.5, (s32[121]{0:T(128)S(1)}, bf16[48,128,128]{2,1,0:T(8,128)(2,1)S(1)}, bf16[48,128,128]{2,1,0:T(8,128)(2,1)S(1)}, f32[8,128]{1,0:T(8,128)S(1)}, ...), branch_computations={%region_0.1_spmd, %region_1.2_spmd, %region_2.3_spmd} | conditional | flops 3347054592 | bytes 56722288 | solution.py:385
  5.8 1.2 %branch_1_fun.11 = (bf16[9,128,128]{2,1,0:T(8,128)(2,1)S(1)}, bf16[9,128,128]{2,1,0:T(8,128)(2,1)S(1)}, bf16[9,128,128]{2,1,0:T(8,128)(2,1)S(1)}, bf16[9,128,128]{2,1,0:T(8,128)(2,1)S(1)}, f32[8,128]{1,0:T(8,128)S(1)}) custom-call(s32[121]{0:T(128)S(1)} %get-tuple-element.118.refs_0_, bf16[48,128,128]{2,1,0:T(8,128)(2,1)S(1)} %get-tuple-element.120.refs_1_, ...), custom_call_target="tpu_custom_call" | custom-call | bytes 4325376 | tf_op jit(solution)/shard_map/cond/branch_1_fun/pallas_call | solution.py:41
  7.0 2.6 %collective-permute-start.17 = (bf16[9,128,128]{2,1,0:T(8,128)(2,1)S(1)}, bf16[9,128,128]{2,1,0:T(8,128)(2,1)S(1)}, u32[]{:S(2)}, u32[]{:S(2)}) collective-permute-start(bf16[9,128,128]{2,1,0:T(8,128)(2,1)S(1)} %get-tuple-element.124), channel_id=1, source_target_pairs={{0,16},{1,17},{2,18},{3,19},{4,20},{5,21},{6,22},{7,23},{8,24},{9,... | collective-permute-start | bytes 884744 | tf_op jit(solution)/shard_map/cond/branch_1_fun/ppermute | solution.py:80
  9.7 1.5 %collective-permute-start.18 = (bf16[9,128,128]{2,1,0:T(8,128)(2,1)S(1)}, bf16[9,128,128]{2,1,0:T(8,128)(2,1)S(1)}, u32[]{:S(2)}, u32[]{:S(2)}) collective-permute-start(bf16[9,128,128]{2,1,0:T(8,128)(2,1)S(1)} %get-tuple-element.125), channel_id=1, source_target_pairs={{0,2},{1,3},{2,0},{3,1},{4,6},{5,7},{6,4},{7,5},{8,10},{9,11},{10,... | collective-permute-start | bytes 884744 | tf_op jit(solution)/shard_map/cond/branch_1_fun/ppermute | solution.py:80
  11.2 0.5 branch_1_fun.12
  11.8 5.4 %collective-permute-done.17.refs_2_ = bf16[9,128,128]{2,1,0:T(8,128)(2,1)S(1)} collective-permute-done((bf16[9,128,128]{2,1,0:T(8,128)(2,1)S(1)}, bf16[9,128,128]{2,1,0:T(8,128)(2,1)S(1)}, u32[]{:S(2)}, u32[]{:S(2)}) %collective-permute-start.17) | collective-permute-done | bytes 294944 | tf_op jit(solution)/shard_map/cond/branch_1_fun/ppermute | solution.py:80
  17.2 2.3 %collective-permute-done.18.refs_3_ = bf16[9,128,128]{2,1,0:T(8,128)(2,1)S(1)} collective-permute-done((bf16[9,128,128]{2,1,0:T(8,128)(2,1)S(1)}, bf16[9,128,128]{2,1,0:T(8,128)(2,1)S(1)}, u32[]{:S(2)}, u32[]{:S(2)}) %collective-permute-start.18) | collective-permute-done | bytes 294944 | tf_op jit(solution)/shard_map/cond/branch_1_fun/ppermute | solution.py:80
  19.5 5.2 %collective-permute-done.19.refs_4_ = bf16[9,128,128]{2,1,0:T(8,128)(2,1)S(1)} collective-permute-done((bf16[9,128,128]{2,1,0:T(8,128)(2,1)S(1)}, bf16[9,128,128]{2,1,0:T(8,128)(2,1)S(1)}, u32[]{:S(2)}, u32[]{:S(2)}) %collective-permute-start.19) | collective-permute-done | bytes 294944 | tf_op jit(solution)/shard_map/cond/branch_1_fun/ppermute | solution.py:80
  24.8 0.7 %branch_1_fun.13 = (bf16[3,128,128]{2,1,0:T(8,128)(2,1)S(1)}, bf16[3,128,128]{2,1,0:T(8,128)(2,1)S(1)}, bf16[3,128,128]{2,1,0:T(8,128)(2,1)S(1)}, bf16[3,128,128]{2,1,0:T(8,128)(2,1)S(1)}, f32[8,128]{1,0:T(8,128)S(1)}) custom-call(s32[121]{0:T(128)S(1)} %get-tuple-element.118.refs_0_, bf16[9,128,128]{2,1,0:T(8,128)(2,1)S(1)} %get-tuple-element.123.refs_1_, ...), custom_call_target="tpu_custom_call" | custom-call | bytes 1572864 | tf_op jit(solution)/shard_map/cond/branch_1_fun/pallas_call | solution.py:41
  25.5 1.8 %collective-permute-start.20 = (bf16[3,128,128]{2,1,0:T(8,128)(2,1)S(1)}, bf16[3,128,128]{2,1,0:T(8,128)(2,1)S(1)}, u32[]{:S(2)}, u32[]{:S(2)}) collective-permute-start(bf16[3,128,128]{2,1,0:T(8,128)(2,1)S(1)} %get-tuple-element.133), channel_id=1, source_target_pairs={{0,4},{1,5},{2,6},{3,7},{4,0},{5,1},{6,2},{7,3},{8,12},{9,13},{10,... | collective-permute-start | bytes 294920 | tf_op jit(solution)/shard_map/cond/branch_1_fun/ppermute | solution.py:80
  27.3 2.6 %collective-permute-start.21 = (bf16[3,128,128]{2,1,0:T(8,128)(2,1)S(1)}, bf16[3,128,128]{2,1,0:T(8,128)(2,1)S(1)}, u32[]{:S(2)}, u32[]{:S(2)}) collective-permute-start(bf16[3,128,128]{2,1,0:T(8,128)(2,1)S(1)} %get-tuple-element.134), channel_id=1, source_target_pairs={{0,8},{1,9},{2,10},{3,11},{4,12},{5,13},{6,14},{7,15},{8,0},{9,1},... | collective-permute-start | bytes 294920 | tf_op jit(solution)/shard_map/cond/branch_1_fun/ppermute | solution.py:80
  30.0 1.2 %collective-permute-done.20.refs_1_ = bf16[3,128,128]{2,1,0:T(8,128)(2,1)S(1)} collective-permute-done((bf16[3,128,128]{2,1,0:T(8,128)(2,1)S(1)}, bf16[3,128,128]{2,1,0:T(8,128)(2,1)S(1)}, u32[]{:S(2)}, u32[]{:S(2)}) %collective-permute-start.20) | collective-permute-done | bytes 98336 | tf_op jit(solution)/shard_map/cond/branch_1_fun/ppermute | solution.py:80
  31.2 5.9 %collective-permute-done.21.refs_2_ = bf16[3,128,128]{2,1,0:T(8,128)(2,1)S(1)} collective-permute-done((bf16[3,128,128]{2,1,0:T(8,128)(2,1)S(1)}, bf16[3,128,128]{2,1,0:T(8,128)(2,1)S(1)}, u32[]{:S(2)}, u32[]{:S(2)}) %collective-permute-start.21) | collective-permute-done | bytes 98336 | tf_op jit(solution)/shard_map/cond/branch_1_fun/ppermute | solution.py:80
  37.2 1.4 %branch_1_fun.15 = (bf16[3,128,128]{2,1,0:T(8,128)(2,1)S(1)}, bf16[3,128,128]{2,1,0:T(8,128)(2,1)S(1)}, f32[8,128]{1,0:T(8,128)S(1)}) custom-call(s32[121]{0:T(128)S(1)} %get-tuple-element.118.refs_0_, f32[1]{0:T(128)} %get-tuple-element.119.refs_1_, bf16[3,128,128]{2,1,0:T(8,128)(2,1)S(1)} %get-tuple-element.137.refs_2_, ...), custom_call_target="tpu_custom_call" | custom-call | flops 176160768 | bytes 3440640 | tf_op jit(solution)/shard_map/cond/branch_1_fun/pallas_call | solution.py:41
  38.6 2.5 %collective-permute-start.25 = (bf16[3,128,128]{2,1,0:T(8,128)(2,1)S(1)}, bf16[3,128,128]{2,1,0:T(8,128)(2,1)S(1)}, u32[]{:S(2)}, u32[]{:S(2)}) collective-permute-start(bf16[3,128,128]{2,1,0:T(8,128)(2,1)S(1)} %get-tuple-element.146.refs_1_), channel_id=1, source_target_pairs={{0,12},{1,13},{2,14},{3,15},{4,8},{5,9},{6,10},{7,11},{8,4},{9,5},... | collective-permute-start | bytes 294920 | tf_op jit(solution)/shard_map/cond/branch_1_fun/ppermute | solution.py:80
  41.1 0.6 collective-permute-start.24
  41.7 1.3 %collective-permute-start.23 = (bf16[3,128,128]{2,1,0:T(8,128)(2,1)S(1)}, bf16[3,128,128]{2,1,0:T(8,128)(2,1)S(1)}, u32[]{:S(2)}, u32[]{:S(2)}) collective-permute-start(bf16[3,128,128]{2,1,0:T(8,128)(2,1)S(1)} %get-tuple-element.146.refs_1_), channel_id=1, source_target_pairs={{0,4},{1,5},{2,6},{3,7},{4,0},{5,1},{6,2},{7,3},{8,12},{9,13},{10,... | collective-permute-start | bytes 294920 | tf_op jit(solution)/shard_map/cond/branch_1_fun/ppermute | solution.py:80
  43.0 1.5 %collective-permute-start.26 = (bf16[3,128,128]{2,1,0:T(8,128)(2,1)S(1)}, bf16[3,128,128]{2,1,0:T(8,128)(2,1)S(1)}, u32[]{:S(2)}, u32[]{:S(2)}) collective-permute-start(bf16[3,128,128]{2,1,0:T(8,128)(2,1)S(1)} %get-tuple-element.147.refs_1_.refs_2_), channel_id=1, source_target_pairs={{0,16},{1,17},{2,18},{3,19},{4,20},{5,21},{6,22},{7,23},{8,24},{9,... | collective-permute-start | bytes 294920 | tf_op jit(solution)/shard_map/cond/branch_1_fun/ppermute | solution.py:80
  44.5 3.7 %branch_1_fun.16 = (f32[3,128,128]{2,1,0:T(8,128)S(1)}, f32[3,128,128]{2,1,0:T(8,128)S(1)}, f32[8,128]{1,0:T(8,128)S(1)}) custom-call(s32[121]{0:T(128)S(1)} %get-tuple-element.118.refs_0_, bf16[3,128,128]{2,1,0:T(8,128)(2,1)S(1)} %get-tuple-element.147.refs_1_.refs_2_, f32[6,128,128]{2,1,0:T(8,128)S(1)} %copy-done.16, f32[6,128,128]{2,1,0:T(8,128)S(1)} %copy-done.19, ...), custom_call_target="tpu_custom_call" | custom-call | flops 1258291200 | bytes 2064384 | tf_op jit(solution)/shard_map/cond/branch_1_fun/pallas_call | solution.py:41
  48.3 0.8 %collective-permute-done.24.refs_3_ = bf16[3,128,128]{2,1,0:T(8,128)(2,1)S(1)} collective-permute-done((bf16[3,128,128]{2,1,0:T(8,128)(2,1)S(1)}, bf16[3,128,128]{2,1,0:T(8,128)(2,1)S(1)}, u32[]{:S(2)}, u32[]{:S(2)}) %collective-permute-start.24) | collective-permute-done | bytes 98336 | tf_op jit(solution)/shard_map/cond/branch_1_fun/ppermute | solution.py:80
  49.1 0.6 branch_1_fun.17
  49.7 2.5 %collective-permute-start.29 = (bf16[9,128,128]{2,1,0:T(8,128)(2,1)S(1)}, bf16[9,128,128]{2,1,0:T(8,128)(2,1)S(1)}, u32[]{:S(2)}, u32[]{:S(2)}) collective-permute-start(bf16[9,128,128]{2,1,0:T(8,128)(2,1)S(1)} %get-tuple-element.152.refs_1_), channel_id=1, source_target_pairs={{0,18},{1,19},{2,16},{3,17},{4,22},{5,23},{6,20},{7,21},{8,26},{9,... | collective-permute-start | bytes 884744 | tf_op jit(solution)/shard_map/cond/branch_1_fun/ppermute | solution.py:80
  52.2 0.5 collective-permute-start.28
  53.3 2.7 %branch_1_fun.18 = (f32[6,128,128]{2,1,0:T(8,128)}, f32[8,128]{1,0:T(8,128)S(1)}) custom-call(s32[121]{0:T(128)S(1)} %get-tuple-element.118.refs_0_, f32[1]{0:T(128)} %get-tuple-element.119.refs_1_, bf16[3,128,128]{2,1,0:T(8,128)(2,1)S(1)} %get-tuple-element.147.refs_1_.refs_2_, bf16[3,128,128]{2,1,0:T(8,128)(2,1)S(1)} %collective-permute-done.26.refs_5_.refs_3_.refs_1_, ...), custom_call_target="tpu_custom_call" | custom-call | flops 452984832 | bytes 3342336 | tf_op jit(solution)/shard_map/cond/branch_1_fun/pallas_call | solution.py:41
  56.0 4.4 %branch_1_fun.19 = (f32[6,128,128]{2,1,0:T(8,128)}, f32[6,128,128]{2,1,0:T(8,128)}, f32[8,128]{1,0:T(8,128)S(1)}) custom-call(s32[121]{0:T(128)S(1)} %get-tuple-element.118.refs_0_, bf16[3,128,128]{2,1,0:T(8,128)(2,1)S(1)} %collective-permute-done.26.refs_5_.refs_3_.refs_1_, f32[6,128,128]{2,1,0:T(8,128)S(1)} %copy-done.16, f32[6,128,128]{2,1,0:T(8,128)S(1)} %copy-done.19, ...), custom_call_target="tpu_custom_call" | custom-call | flops 1258291200 | bytes 2850816 | tf_op jit(solution)/shard_map/cond/branch_1_fun/pallas_call | solution.py:41
  61.0 3.7 %collective-permute-done.28.refs_3_ = bf16[9,128,128]{2,1,0:T(8,128)(2,1)S(1)} collective-permute-done((bf16[9,128,128]{2,1,0:T(8,128)(2,1)S(1)}, bf16[9,128,128]{2,1,0:T(8,128)(2,1)S(1)}, u32[]{:S(2)}, u32[]{:S(2)}) %collective-permute-start.28) | collective-permute-done | bytes 294944 | tf_op jit(solution)/shard_map/cond/branch_1_fun/ppermute | solution.py:80
  64.6 0.5 collective-permute-start.31
  65.2 1.1 %collective-permute-done.32.refs_7_ = bf16[9,128,128]{2,1,0:T(8,128)(2,1)S(1)} collective-permute-done((bf16[9,128,128]{2,1,0:T(8,128)(2,1)S(1)}, bf16[9,128,128]{2,1,0:T(8,128)(2,1)S(1)}, u32[]{:S(2)}, u32[]{:S(2)}) %collective-permute-start.32) | collective-permute-done | bytes 294944 | tf_op jit(solution)/shard_map/cond/branch_1_fun/ppermute | solution.py:80
  66.6 2.3 %branch_1_fun.21 = (bf16[48,128,128]{2,1,0:T(8,128)(2,1)}, f32[8,128]{1,0:T(8,128)}) custom-call(s32[121]{0:T(128)S(1)} %get-tuple-element.118.refs_0_, bf16[9,128,128]{2,1,0:T(8,128)(2,1)S(1)} %get-tuple-element.152.refs_1_, bf16[9,128,128]{2,1,0:T(8,128)(2,1)S(1)} %collective-permute-done.27.refs_2_, ...), custom_call_target="tpu_custom_call" | custom-call | bytes 3932160 | tf_op jit(solution)/shard_map/cond/branch_1_fun/pallas_call | solution.py:41
  (37 shorter events, 2.0 us)
Async XLA Ops:
  0.6 2.8 %copy-start.1 = (s32[48]{0:T(128)S(1)}, s32[48]{0:T(128)}, u32[]{:S(2)}) copy-start(s32[48]{0:T(128)} %refs_1_.1) | copy-start | bytes 580
  0.6 5.1 %collective-permute-start.51 = (bf16[48,128,128]{2,1,0:T(8,128)(2,1)}, bf16[48,128,128]{2,1,0:T(8,128)(2,1)S(1)}, u32[]{:S(2)}, u32[]{:S(2)}) collective-permute-start(bf16[48,128,128]{2,1,0:T(8,128)(2,1)} %bitcast.6), channel_id=1, source_target_pairs={{0,1},{1,0},{2,3},{3,2},{4,5},{5,4},{6,7},{7,6},{8,9},{9,8},{10,11... | collective-permute-start | bytes 4718600 | tf_op jit(solution)/shard_map/ppermute | solution.py:80
  1.2 1.4 %copy-start = (bf16[1,48,128,128]{3,2,1,0:T(8,128)(2,1)S(1)}, bf16[1,48,128,128]{3,2,1,0:T(8,128)(2,1)}, u32[]{:S(2)}) copy-start(bf16[1,48,128,128]{3,2,1,0:T(8,128)(2,1)} %param.13) | copy-start | bytes 4718596
  2.6 3.2 %copy-start.2 = (f32[6,128,128]{2,1,0:T(8,128)S(1)}, f32[6,128,128]{2,1,0:T(8,128)}, u32[]{:S(2)}) copy-start(f32[6,128,128]{2,1,0:T(8,128)} %param.18) | copy-start | bytes 1179652
  5.8 5.5 %copy-start.7 = (f32[6,128,128]{2,1,0:T(8,128)S(1)}, f32[6,128,128]{2,1,0:T(8,128)}, u32[]{:S(2)}) copy-start(f32[6,128,128]{2,1,0:T(8,128)} %get-tuple-element.127.refs_0_) | copy-start | bytes 1179652 | tf_op jit(solution)/shard_map/cond
  5.8 5.5 %copy-start.10 = (f32[6,128,128]{2,1,0:T(8,128)S(1)}, f32[6,128,128]{2,1,0:T(8,128)}, u32[]{:S(2)}) copy-start(f32[6,128,128]{2,1,0:T(8,128)} %get-tuple-element.128.refs_1_.refs_4_) | copy-start | bytes 1179652 | tf_op jit(solution)/shard_map/cond
  5.8 5.4 %copy-start.13 = (f32[6,128,128]{2,1,0:T(8,128)S(1)}, f32[6,128,128]{2,1,0:T(8,128)}, u32[]{:S(2)}) copy-start(f32[6,128,128]{2,1,0:T(8,128)} %get-tuple-element.129.refs_2_.refs_5_) | copy-start | bytes 1179652 | tf_op jit(solution)/shard_map/cond
  7.0 30.1 %copy-start.4 = (f32[6,128,128]{2,1,0:T(8,128)S(1)}, f32[6,128,128]{2,1,0:T(8,128)}, u32[]{:S(2)}) copy-start(f32[6,128,128]{2,1,0:T(8,128)} %get-tuple-element.140.refs_5_) | copy-start | bytes 1179652 | tf_op jit(solution)/shard_map/cond
  7.0 10.1 %collective-permute-start.17 = (bf16[9,128,128]{2,1,0:T(8,128)(2,1)S(1)}, bf16[9,128,128]{2,1,0:T(8,128)(2,1)S(1)}, u32[]{:S(2)}, u32[]{:S(2)}) collective-permute-start(bf16[9,128,128]{2,1,0:T(8,128)(2,1)S(1)} %get-tuple-element.124), channel_id=1, source_target_pairs={{0,16},{1,17},{2,18},{3,19},{4,20},{5,21},{6,22},{7,23},{8,24},{9,... | collective-permute-start | bytes 884744 | tf_op jit(solution)/shard_map/cond/branch_1_fun/ppermute | solution.py:80
  9.7 9.9 %collective-permute-start.18 = (bf16[9,128,128]{2,1,0:T(8,128)(2,1)S(1)}, bf16[9,128,128]{2,1,0:T(8,128)(2,1)S(1)}, u32[]{:S(2)}, u32[]{:S(2)}) collective-permute-start(bf16[9,128,128]{2,1,0:T(8,128)(2,1)S(1)} %get-tuple-element.125), channel_id=1, source_target_pairs={{0,2},{1,3},{2,0},{3,1},{4,6},{5,7},{6,4},{7,5},{8,10},{9,11},{10,... | collective-permute-start | bytes 884744 | tf_op jit(solution)/shard_map/cond/branch_1_fun/ppermute | solution.py:80
  11.2 13.6 %collective-permute-start.19 = (bf16[9,128,128]{2,1,0:T(8,128)(2,1)S(1)}, bf16[9,128,128]{2,1,0:T(8,128)(2,1)S(1)}, u32[]{:S(2)}, u32[]{:S(2)}) collective-permute-start(bf16[9,128,128]{2,1,0:T(8,128)(2,1)S(1)} %get-tuple-element.126), channel_id=1, source_target_pairs={{0,18},{1,19},{2,16},{3,17},{4,22},{5,23},{6,20},{7,21},{8,26},{9,... | collective-permute-start | bytes 884744 | tf_op jit(solution)/shard_map/cond/branch_1_fun/ppermute | solution.py:80
  25.5 5.7 %collective-permute-start.20 = (bf16[3,128,128]{2,1,0:T(8,128)(2,1)S(1)}, bf16[3,128,128]{2,1,0:T(8,128)(2,1)S(1)}, u32[]{:S(2)}, u32[]{:S(2)}) collective-permute-start(bf16[3,128,128]{2,1,0:T(8,128)(2,1)S(1)} %get-tuple-element.133), channel_id=1, source_target_pairs={{0,4},{1,5},{2,6},{3,7},{4,0},{5,1},{6,2},{7,3},{8,12},{9,13},{10,... | collective-permute-start | bytes 294920 | tf_op jit(solution)/shard_map/cond/branch_1_fun/ppermute | solution.py:80
  27.3 9.8 %collective-permute-start.21 = (bf16[3,128,128]{2,1,0:T(8,128)(2,1)S(1)}, bf16[3,128,128]{2,1,0:T(8,128)(2,1)S(1)}, u32[]{:S(2)}, u32[]{:S(2)}) collective-permute-start(bf16[3,128,128]{2,1,0:T(8,128)(2,1)S(1)} %get-tuple-element.134), channel_id=1, source_target_pairs={{0,8},{1,9},{2,10},{3,11},{4,12},{5,13},{6,14},{7,15},{8,0},{9,1},... | collective-permute-start | bytes 294920 | tf_op jit(solution)/shard_map/cond/branch_1_fun/ppermute | solution.py:80
  29.9 7.2 %collective-permute-start.22 = (bf16[3,128,128]{2,1,0:T(8,128)(2,1)S(1)}, bf16[3,128,128]{2,1,0:T(8,128)(2,1)S(1)}, u32[]{:S(2)}, u32[]{:S(2)}) collective-permute-start(bf16[3,128,128]{2,1,0:T(8,128)(2,1)S(1)} %get-tuple-element.135), channel_id=1, source_target_pairs={{0,12},{1,13},{2,14},{3,15},{4,8},{5,9},{6,10},{7,11},{8,4},{9,5},... | collective-permute-start | bytes 294920 | tf_op jit(solution)/shard_map/cond/branch_1_fun/ppermute | solution.py:80
  37.2 7.4 %copy-start.16 = (f32[6,128,128]{2,1,0:T(8,128)S(1)}, f32[6,128,128]{2,1,0:T(8,128)}, u32[]{:S(2)}) copy-start(f32[6,128,128]{2,1,0:T(8,128)} %get-tuple-element.148.refs_2_) | copy-start | bytes 1179652 | tf_op jit(solution)/shard_map/cond
  37.2 7.4 %copy-start.19 = (f32[6,128,128]{2,1,0:T(8,128)S(1)}, f32[6,128,128]{2,1,0:T(8,128)}, u32[]{:S(2)}) copy-start(f32[6,128,128]{2,1,0:T(8,128)} %get-tuple-element.149.refs_3_) | copy-start | bytes 1179652 | tf_op jit(solution)/shard_map/cond
  38.6 9.7 %collective-permute-start.25 = (bf16[3,128,128]{2,1,0:T(8,128)(2,1)S(1)}, bf16[3,128,128]{2,1,0:T(8,128)(2,1)S(1)}, u32[]{:S(2)}, u32[]{:S(2)}) collective-permute-start(bf16[3,128,128]{2,1,0:T(8,128)(2,1)S(1)} %get-tuple-element.146.refs_1_), channel_id=1, source_target_pairs={{0,12},{1,13},{2,14},{3,15},{4,8},{5,9},{6,10},{7,11},{8,4},{9,5},... | collective-permute-start | bytes 294920 | tf_op jit(solution)/shard_map/cond/branch_1_fun/ppermute | solution.py:80
  41.1 8.0 %collective-permute-start.24 = (bf16[3,128,128]{2,1,0:T(8,128)(2,1)S(1)}, bf16[3,128,128]{2,1,0:T(8,128)(2,1)S(1)}, u32[]{:S(2)}, u32[]{:S(2)}) collective-permute-start(bf16[3,128,128]{2,1,0:T(8,128)(2,1)S(1)} %get-tuple-element.146.refs_1_), channel_id=1, source_target_pairs={{0,8},{1,9},{2,10},{3,11},{4,12},{5,13},{6,14},{7,15},{8,0},{9,1},... | collective-permute-start | bytes 294920 | tf_op jit(solution)/shard_map/cond/branch_1_fun/ppermute | solution.py:80
  41.7 7.4 %collective-permute-start.23 = (bf16[3,128,128]{2,1,0:T(8,128)(2,1)S(1)}, bf16[3,128,128]{2,1,0:T(8,128)(2,1)S(1)}, u32[]{:S(2)}, u32[]{:S(2)}) collective-permute-start(bf16[3,128,128]{2,1,0:T(8,128)(2,1)S(1)} %get-tuple-element.146.refs_1_), channel_id=1, source_target_pairs={{0,4},{1,5},{2,6},{3,7},{4,0},{5,1},{6,2},{7,3},{8,12},{9,13},{10,... | collective-permute-start | bytes 294920 | tf_op jit(solution)/shard_map/cond/branch_1_fun/ppermute | solution.py:80
  43.0 5.3 %collective-permute-start.26 = (bf16[3,128,128]{2,1,0:T(8,128)(2,1)S(1)}, bf16[3,128,128]{2,1,0:T(8,128)(2,1)S(1)}, u32[]{:S(2)}, u32[]{:S(2)}) collective-permute-start(bf16[3,128,128]{2,1,0:T(8,128)(2,1)S(1)} %get-tuple-element.147.refs_1_.refs_2_), channel_id=1, source_target_pairs={{0,16},{1,17},{2,18},{3,19},{4,20},{5,21},{6,22},{7,23},{8,24},{9,... | collective-permute-start | bytes 294920 | tf_op jit(solution)/shard_map/cond/branch_1_fun/ppermute | solution.py:80
  49.7 11.0 %collective-permute-start.29 = (bf16[9,128,128]{2,1,0:T(8,128)(2,1)S(1)}, bf16[9,128,128]{2,1,0:T(8,128)(2,1)S(1)}, u32[]{:S(2)}, u32[]{:S(2)}) collective-permute-start(bf16[9,128,128]{2,1,0:T(8,128)(2,1)S(1)} %get-tuple-element.152.refs_1_), channel_id=1, source_target_pairs={{0,18},{1,19},{2,16},{3,17},{4,22},{5,23},{6,20},{7,21},{8,26},{9,... | collective-permute-start | bytes 884744 | tf_op jit(solution)/shard_map/cond/branch_1_fun/ppermute | solution.py:80
  52.2 12.4 %collective-permute-start.28 = (bf16[9,128,128]{2,1,0:T(8,128)(2,1)S(1)}, bf16[9,128,128]{2,1,0:T(8,128)(2,1)S(1)}, u32[]{:S(2)}, u32[]{:S(2)}) collective-permute-start(bf16[9,128,128]{2,1,0:T(8,128)(2,1)S(1)} %get-tuple-element.152.refs_1_), channel_id=1, source_target_pairs={{0,2},{1,3},{2,0},{3,1},{4,6},{5,7},{6,4},{7,5},{8,10},{9,11},{10,... | collective-permute-start | bytes 884744 | tf_op jit(solution)/shard_map/cond/branch_1_fun/ppermute | solution.py:80
  52.8 11.9 %collective-permute-start.27 = (bf16[9,128,128]{2,1,0:T(8,128)(2,1)S(1)}, bf16[9,128,128]{2,1,0:T(8,128)(2,1)S(1)}, u32[]{:S(2)}, u32[]{:S(2)}) collective-permute-start(bf16[9,128,128]{2,1,0:T(8,128)(2,1)S(1)} %get-tuple-element.152.refs_1_), channel_id=1, source_target_pairs={{0,16},{1,17},{2,18},{3,19},{4,20},{5,21},{6,22},{7,23},{8,24},{9,... | collective-permute-start | bytes 884744 | tf_op jit(solution)/shard_map/cond/branch_1_fun/ppermute | solution.py:80
  53.3 11.9 %collective-permute-start.30 = (bf16[9,128,128]{2,1,0:T(8,128)(2,1)S(1)}, bf16[9,128,128]{2,1,0:T(8,128)(2,1)S(1)}, u32[]{:S(2)}, u32[]{:S(2)}) collective-permute-start(bf16[9,128,128]{2,1,0:T(8,128)(2,1)S(1)} %get-tuple-element.152.refs_1_), channel_id=1, source_target_pairs={{0,1},{1,0},{2,3},{3,2},{4,5},{5,4},{6,7},{7,6},{8,9},{9,8},{10,11... | collective-permute-start | bytes 884744 | tf_op jit(solution)/shard_map/cond/branch_1_fun/ppermute | solution.py:80
  60.7 4.5 %collective-permute-start.33 = (bf16[9,128,128]{2,1,0:T(8,128)(2,1)S(1)}, bf16[9,128,128]{2,1,0:T(8,128)(2,1)S(1)}, u32[]{:S(2)}, u32[]{:S(2)}) collective-permute-start(bf16[9,128,128]{2,1,0:T(8,128)(2,1)S(1)} %get-tuple-element.158.refs_4_), channel_id=1, source_target_pairs={{0,1},{1,0},{2,3},{3,2},{4,5},{5,4},{6,7},{7,6},{8,9},{9,8},{10,11... | collective-permute-start | bytes 884744 | tf_op jit(solution)/shard_map/cond/branch_1_fun/ppermute | solution.py:80
  64.6 1.6 %collective-permute-start.32 = (bf16[9,128,128]{2,1,0:T(8,128)(2,1)S(1)}, bf16[9,128,128]{2,1,0:T(8,128)(2,1)S(1)}, u32[]{:S(2)}, u32[]{:S(2)}) collective-permute-start(bf16[9,128,128]{2,1,0:T(8,128)(2,1)S(1)} %collective-permute-done.28.refs_3_), channel_id=1, source_target_pairs={{0,1},{1,0},{2,3},{3,2},{4,5},{5,4},{6,7},{7,6},{8,9},{9,8},{10,11... | collective-permute-start | bytes 884744 | tf_op jit(solution)/shard_map/cond/branch_1_fun/ppermute | solution.py:80
  64.6 2.0 %collective-permute-start.31 = (bf16[9,128,128]{2,1,0:T(8,128)(2,1)S(1)}, bf16[9,128,128]{2,1,0:T(8,128)(2,1)S(1)}, u32[]{:S(2)}, u32[]{:S(2)}) collective-permute-start(bf16[9,128,128]{2,1,0:T(8,128)(2,1)S(1)} %collective-permute-done.27.refs_2_), channel_id=1, source_target_pairs={{0,1},{1,0},{2,3},{3,2},{4,5},{5,4},{6,7},{7,6},{8,9},{9,8},{10,11... | collective-permute-start | bytes 884744 | tf_op jit(solution)/shard_map/cond/branch_1_fun/ppermute | solution.py:80
